TPU v7x, 256 devices: a whole 4x4x8 slice. The times are simulated.
256 devices in a mesh: ctx: 128 (over y, z, x), head: 2 (over core).
Axes of the slice: x: 4, y: 4, z: 8, core: 2. Of those that a mesh axis runs over, the one named last changes fastest.
Arguments:
- queries: bfloat16 [32768, 2560], P('ctx', 'head'), may hold values from -30 to 30
- keys: bfloat16 [32768, 512], P('ctx', 'head'), may hold values from -6 to 6
- values: bfloat16 [32768, 512], P('ctx', 'head'), may hold values from -6 to 6
- far_owners: int32 [256, 16], P('ctx'), may hold values from 0 to 127, as said below
- far_counts: int32 [256], P('ctx'), may hold values from 0 to 16, as said below
- pair_blocks: int32 [64, 128], replicated, may hold values from 0 to 255, as said below
Outputs:
- attended: bfloat16 [32768, 2560], P(('ctx', 'head'))
Inputs may be any that keep to these rules, and one draw needn't show every extreme that they name: `far_owners`: entries j < far_counts[r] of row r are distinct shards before the shard that holds block r; the other entries are arbitrary shards. far_counts[r] is at most the index of the shard that holds block r. `pair_blocks`: entry [p, o] is a block held by shard o.
All inputs are finite; a program needn't handle non-finite values.
Results may differ from a plain program's by a relative error of at most 0.0049.
Values may be sent and summed in bfloat16 or wider, within the bound.
A program may use at most 128 MiB of HBM per device.

v0:
```python
import jax
import jax.numpy as jnp
from jax import lax
from jax.sharding import PartitionSpec as P

HEAD_WIDTH = 128
BLOCK_TOKENS = 128


tiles_per_step = 4


def tile_list(step_index, local_row, base_tile, owners, far_count, far_start):
    slot_ids = step_index * tiles_per_step + jnp.arange(tiles_per_step, dtype=jnp.int32)
    tile_total = local_row + 1 + far_count
    far_slot = jnp.clip(slot_ids - local_row - 1, 0, owners.shape[0] - 1)
    tile_ids = jnp.where(slot_ids <= local_row, base_tile + slot_ids, far_start + owners[far_slot])
    is_valid = slot_ids < tile_total
    return (jnp.where(is_valid, tile_ids, base_tile), slot_ids, is_valid)


def attend_head(
    query_head,
    head_index,
    local_row,
    base_tile,
    owners,
    far_count,
    pool_keys,
    pool_values,
    far_start,
    step_limit,
):
    block_rows = query_head.shape[1]
    group_width = query_head.shape[0]
    score_scale = HEAD_WIDTH ** (-0.5)
    step_count = (local_row + 1 + far_count + tiles_per_step - 1) // tiles_per_step
    query_pos = local_row * block_rows + jnp.arange(block_rows, dtype=jnp.int32)
    token_ids = jnp.arange(block_rows, dtype=jnp.int32)

    def tile_rows(pool, tile_ids):
        selected_blocks = jnp.take(pool, tile_ids, axis=0)
        selected_blocks = lax.dynamic_slice_in_dim(
            selected_blocks, head_index * HEAD_WIDTH, HEAD_WIDTH, 2
        )
        return selected_blocks.reshape(tiles_per_step * block_rows, HEAD_WIDTH)

    def first_pass(step_index, running):
        stored_scores, row_top, exp_total = running
        tile_ids, slot_ids, is_valid = tile_list(
            step_index, local_row, base_tile, owners, far_count, far_start
        )
        keys_now = tile_rows(pool_keys, tile_ids)
        scores = (
            jnp.einsum("gqd,kd->gqk", query_head, keys_now, preferred_element_type=jnp.float32)
            * score_scale
        )
        key_pos = (slot_ids[:, None] * block_rows + token_ids[None, :]).reshape(-1)
        is_local = jnp.repeat(slot_ids <= local_row, block_rows)
        is_live = jnp.repeat(is_valid, block_rows)
        visible = is_live[None, :] & (
            jnp.logical_not(is_local)[None, :] | (key_pos[None, :] <= query_pos[:, None])
        )
        scores = jnp.where(visible[None], scores, -jnp.inf)
        new_top = jnp.maximum(row_top, scores.max(-1))
        exp_total = exp_total * jnp.exp(row_top - new_top) + jnp.exp(
            scores - new_top[..., None]
        ).sum(-1)
        stored_scores = lax.dynamic_update_index_in_dim(stored_scores, scores, step_index, 0)
        return (stored_scores, new_top, exp_total)

    start_state = (
        jnp.zeros((step_limit, group_width, block_rows, tiles_per_step * block_rows), jnp.float32),
        jnp.full((group_width, block_rows), -jnp.inf, jnp.float32),
        jnp.zeros((group_width, block_rows), jnp.float32),
    )
    stored_scores, row_top, exp_total = lax.fori_loop(0, step_count, first_pass, start_state)

    def second_pass(step_index, output_sum):
        tile_ids, slot_ids, is_valid = tile_list(
            step_index, local_row, base_tile, owners, far_count, far_start
        )
        scores = lax.dynamic_index_in_dim(stored_scores, step_index, 0, keepdims=False)
        weights = (jnp.exp(scores - row_top[..., None]) / exp_total[..., None]).astype(jnp.bfloat16)
        values_now = tile_rows(pool_values, tile_ids)
        return output_sum + jnp.einsum(
            "gqk,kd->qgd", weights, values_now, preferred_element_type=jnp.float32
        )

    output_sum = lax.fori_loop(
        0, step_count, second_pass, jnp.zeros((block_rows, group_width, HEAD_WIDTH), jnp.float32)
    )
    return output_sum.astype(jnp.bfloat16)


def attend_rows(
    query_rows,
    local_rows,
    base_tiles,
    owners,
    far_counts,
    pool_keys,
    pool_values,
    far_start,
    step_limit,
):
    block_rows = query_rows.shape[1]
    kv_heads = pool_keys.shape[2] // HEAD_WIDTH
    group_width = query_rows.shape[2] // (kv_heads * HEAD_WIDTH)

    def one_row(row_items):
        query_block_index, local_row, base_tile, row_owners, far_count = row_items
        grouped = query_block_index.reshape(block_rows, kv_heads, group_width, HEAD_WIDTH)

        def one_head(head_index):
            query_head = jnp.moveaxis(
                lax.dynamic_index_in_dim(grouped, head_index, 1, keepdims=False), 1, 0
            )
            return attend_head(
                query_head,
                head_index,
                local_row,
                base_tile,
                row_owners,
                far_count,
                pool_keys,
                pool_values,
                far_start,
                step_limit,
            )

        head_outputs = lax.map(one_head, jnp.arange(kv_heads, dtype=jnp.int32))
        return jnp.moveaxis(head_outputs, 0, 1).reshape(block_rows, -1)

    return lax.map(one_row, (query_rows, local_rows, base_tiles, owners, far_counts))


def on_device(queries, keys, values, far_owners, far_counts, pair_blocks):
    shards = lax.axis_size("ctx")
    device_index = lax.axis_index("ctx")
    tokens = queries.shape[0]
    blocks = tokens // BLOCK_TOKENS
    key_width = keys.shape[1]
    targets = jnp.arange(shards, dtype=jnp.int32)
    partners = jnp.minimum(targets, shards - 1 - targets)
    column = lax.dynamic_index_in_dim(pair_blocks, device_index, 1, keepdims=False)
    chosen = jnp.take(column, partners) - device_index * blocks
    key_blocks = keys.reshape(blocks, BLOCK_TOKENS, key_width)
    value_blocks = values.reshape(blocks, BLOCK_TOKENS, key_width)
    candidate_keys, candidate_values = (
        lax.all_to_all(
            jnp.take(key_blocks, chosen, axis=0), "ctx", split_axis=0, concat_axis=0, tiled=True
        ),
        lax.all_to_all(
            jnp.take(value_blocks, chosen, axis=0), "ctx", split_axis=0, concat_axis=0, tiled=True
        ),
    )
    query_rows = queries.reshape(blocks, BLOCK_TOKENS, queries.shape[1])
    step_limit = (blocks + far_owners.shape[1] + tiles_per_step - 1) // tiles_per_step
    row_ids = jnp.arange(blocks, dtype=jnp.int32)
    pool_keys = jnp.concatenate([key_blocks, candidate_keys], 0)
    pool_values = jnp.concatenate([value_blocks, candidate_values], 0)
    attended = attend_rows(
        query_rows,
        row_ids,
        jnp.zeros_like(row_ids),
        far_owners,
        far_counts,
        pool_keys,
        pool_values,
        blocks,
        step_limit,
    )
    result = attended.reshape(tokens, -1)
    return lax.all_to_all(result, "head", split_axis=0, concat_axis=1, tiled=True)


def solution(mesh):
    placed = (P("ctx", "head"), P("ctx", "head"), P("ctx", "head"), P("ctx", None), P("ctx"), P())
    return jax.shard_map(
        on_device, mesh=mesh, in_specs=placed, out_specs=P(("ctx", "head"), None), check_vma=False
    )
```

profile of v0, /device:TPU:249, one launch (start us, length us, event | category | flops | bytes accessed | tf_op | source)
XLA Modules:
  0.0 808.6 jit_solution(14785479762648484670)
XLA Ops:
  2.2 7.3 gather_fusion.5
  9.5 6.4 gather_fusion.6
  15.9 9.4 %broadcast_select_fusion = (bf16[128,128,256]{2,1,0:T(8,128)(2,1)}, bf16[128,128,256]{2,1,0:T(8,128)(2,1)S(1)}) fusion(bf16[128,128,256]{2,1,0:T(8,128)(2,1)} %gather_fusion.6, pred[128]{0:T(512)(128)(4,1)S(1)} %get-tuple-element.1133, bf16[128,128,256]{2,1,0:T(8,128)(2,1)} %gather_fusion.5), kind=kLoop, calls=%fused_computation.56 | loop fusion | flops 8388608 | bytes 33554560 | tf_op jit(solution)/shard_map/jit(_take)/select_n | solution.py:155
  25.3 194.3 %all_to_all.26 = bf16[128,128,256]{2,1,0:T(8,128)(2,1)} all-to-all(bf16[128,128,256]{2,1,0:T(8,128)(2,1)S(1)} %get-tuple-element.1139), channel_id=1, replica_groups=mesh['ctx'=128,'head'=2] {'ctx'}, dimensions={0} | all-to-all | bytes 16777216 | tf_op jit(solution)/shard_map/all_to_all | solution.py:151
  219.6 12.1 %all-to-all-start.1 = ((bf16[128,128,256]{2,1,0:T(8,128)(2,1)}), bf16[128,128,256]{2,1,0:T(8,128)(2,1)}, u32[]{:S(2)}, u32[]{:S(2)}) async-start(bf16[128,128,256]{2,1,0:T(8,128)(2,1)} %get-tuple-element.1138), calls=%async_computation.1 | async-start | bytes 16777216 | tf_op jit(solution)/shard_map/all_to_all | solution.py:154
  231.7 7.4 pad_maximum_fusion
  239.1 172.7 %all-to-all-done.1 = bf16[128,128,256]{2,1,0:T(8,128)(2,1)} async-done(((bf16[128,128,256]{2,1,0:T(8,128)(2,1)}), bf16[128,128,256]{2,1,0:T(8,128)(2,1)}, u32[]{:S(2)}, u32[]{:S(2)}) %all-to-all-start.1) | async-done | bytes 8388640 | tf_op jit(solution)/shard_map/all_to_all | solution.py:154
  411.9 7.4 pad_maximum_fusion.1
  419.2 378.3 %while.105 = (s32[]{:T(128)}, bf16[2,128,1280]{1,2,0:T(8,128)(2,1)}, bf16[2,128,1280]{2,1,0:T(8,128)(2,1)}, s32[2]{0:T(128)S(1)}, s32[2]{0:T(128)S(1)}, /*index=...) while((s32[]{:T(128)}, bf16[2,128,1280]{1,2,0:T(8,128)(2,1)}, ...), condition=%wide.region_9.12_spmd, body=%wide.region_0.11_spmd.sunk | while | flops 170891344 | bytes 24646388 | solution.py:135
  423.7 183.0 %while.106 = (s32[]{:T(128)}, bf16[2,128,5,128]{1,3,2,0:T(8,128)(2,1)}, s32[2]{0:T(128)S(1)}, bf16[128,2,5,128]{0,3,2,1:T(8,128)(2,1)S(1)}, s32[]{:T(128)}, /*in...) while((s32[]{:T(128)}, ...), condition=%wide.region_8.10_spmd, body=%wide.region_1.9_spmd.sunk | while | flops 170891328 | bytes 22678944 | solution.py:132
  430.5 41.7 %while.107 = (s32[]{:T(128)}, f32[5,5,128,512]{2,3,1,0:T(8,128)}, f32[5,128]{1,0:T(8,128)S(1)}, f32[5,128]{1,0:T(8,128)S(1)}, s32[]{:T(128)}, /*index=5*/s32[]{:...) while((s32[]{:T(128)}, f32[5,5,128,512]{2,3,1,0:T(8,128)}, ...), condition=%wide.region_5.6_spmd.clone, body=%wide.region_2.5_spmd.clone.sunk | while | flops 85790696 | bytes 6504387 | solution.py:77
  432.5 4.0 gather_fusion.1
  440.8 4.0 gather_fusion.1
  449.1 4.0 gather_fusion.1
  457.4 4.0 gather_fusion.1
  465.8 4.0 gather_fusion.1
  472.2 42.3 %while.108 = (s32[]{:T(128)}, f32[128,5,128]{0,2,1:T(8,128)S(1)}, s32[]{:T(128)}, s32[]{:T(128)}, s32[]{:T(128)}, /*index=5*/s32[16]{0:T(128)S(1)}, bf16[130,128...) while((s32[]{:T(128)}, f32[128,5,128]{0,2,1:T(8,128)S(1)}, ...), condition=%wide.region_7.8_spmd, body=%wide.region_6.7_spmd.sunk | while | flops 85018704 | bytes 8140143 | solution.py:90
  474.2 4.0 gather_fusion.3
  482.6 4.0 gather_fusion.3
  491.1 4.0 gather_fusion.3
  499.5 4.0 gather_fusion.3
  508.0 4.0 gather_fusion.3
  522.0 41.7 %while.107 = (s32[]{:T(128)}, f32[5,5,128,512]{2,3,1,0:T(8,128)}, f32[5,128]{1,0:T(8,128)S(1)}, f32[5,128]{1,0:T(8,128)S(1)}, s32[]{:T(128)}, /*index=5*/s32[]{:...) while((s32[]{:T(128)}, f32[5,5,128,512]{2,3,1,0:T(8,128)}, ...), condition=%wide.region_5.6_spmd.clone, body=%wide.region_2.5_spmd.clone.sunk | while | flops 85790696 | bytes 6504387 | solution.py:77
  523.9 4.0 gather_fusion.1
  532.3 4.0 gather_fusion.1
  540.6 4.0 gather_fusion.1
  548.9 4.0 gather_fusion.1
  557.3 4.0 gather_fusion.1
  563.7 42.3 %while.108 = (s32[]{:T(128)}, f32[128,5,128]{0,2,1:T(8,128)S(1)}, s32[]{:T(128)}, s32[]{:T(128)}, s32[]{:T(128)}, /*index=5*/s32[16]{0:T(128)S(1)}, bf16[130,128...) while((s32[]{:T(128)}, f32[128,5,128]{0,2,1:T(8,128)S(1)}, ...), condition=%wide.region_7.8_spmd, body=%wide.region_6.7_spmd.sunk | while | flops 85018704 | bytes 8140143 | solution.py:90
  565.7 4.0 gather_fusion.3
  574.1 4.0 gather_fusion.3
  582.6 4.0 gather_fusion.3
  591.0 4.0 gather_fusion.3
  599.5 4.0 gather_fusion.3
  612.8 183.0 %while.106 = (s32[]{:T(128)}, bf16[2,128,5,128]{1,3,2,0:T(8,128)(2,1)}, s32[2]{0:T(128)S(1)}, bf16[128,2,5,128]{0,3,2,1:T(8,128)(2,1)S(1)}, s32[]{:T(128)}, /*in...) while((s32[]{:T(128)}, ...), condition=%wide.region_8.10_spmd, body=%wide.region_1.9_spmd.sunk | while | flops 170891328 | bytes 22678944 | solution.py:132
  619.6 41.7 %while.107 = (s32[]{:T(128)}, f32[5,5,128,512]{2,3,1,0:T(8,128)}, f32[5,128]{1,0:T(8,128)S(1)}, f32[5,128]{1,0:T(8,128)S(1)}, s32[]{:T(128)}, /*index=5*/s32[]{:...) while((s32[]{:T(128)}, f32[5,5,128,512]{2,3,1,0:T(8,128)}, ...), condition=%wide.region_5.6_spmd.clone, body=%wide.region_2.5_spmd.clone.sunk | while | flops 85790696 | bytes 6504387 | solution.py:77
  621.6 4.0 gather_fusion.1
  629.9 4.0 gather_fusion.1
  638.3 4.0 gather_fusion.1
  646.6 4.0 gather_fusion.1
  661.4 42.3 %while.108 = (s32[]{:T(128)}, f32[128,5,128]{0,2,1:T(8,128)S(1)}, s32[]{:T(128)}, s32[]{:T(128)}, s32[]{:T(128)}, /*index=5*/s32[16]{0:T(128)S(1)}, bf16[130,128...) while((s32[]{:T(128)}, f32[128,5,128]{0,2,1:T(8,128)S(1)}, ...), condition=%wide.region_7.8_spmd, body=%wide.region_6.7_spmd.sunk | while | flops 85018704 | bytes 8140143 | solution.py:90
  697.1 4.0 gather_fusion.3
  711.1 41.7 %while.107 = (s32[]{:T(128)}, f32[5,5,128,512]{2,3,1,0:T(8,128)}, f32[5,128]{1,0:T(8,128)S(1)}, f32[5,128]{1,0:T(8,128)S(1)}, s32[]{:T(128)}, /*index=5*/s32[]{:...) while((s32[]{:T(128)}, f32[5,5,128,512]{2,3,1,0:T(8,128)}, ...), condition=%wide.region_5.6_spmd.clone, body=%wide.region_2.5_spmd.clone.sunk | while | flops 85790696 | bytes 6504387 | solution.py:77
  738.1 4.0 gather_fusion.1
  752.8 42.3 %while.108 = (s32[]{:T(128)}, f32[128,5,128]{0,2,1:T(8,128)S(1)}, s32[]{:T(128)}, s32[]{:T(128)}, s32[]{:T(128)}, /*index=5*/s32[16]{0:T(128)S(1)}, bf16[130,128...) while((s32[]{:T(128)}, f32[128,5,128]{0,2,1:T(8,128)S(1)}, ...), condition=%wide.region_7.8_spmd, body=%wide.region_6.7_spmd.sunk | while | flops 85018704 | bytes 8140143 | solution.py:90
  771.7 4.0 gather_fusion.3
  780.2 4.0 gather_fusion.3
  797.5 10.0 %all_to_all.27 = bf16[2,128,1280]{1,2,0:T(8,128)(2,1)S(1)} all-to-all(bf16[2,128,1280]{1,2,0:T(8,128)(2,1)} %get-tuple-element.952), channel_id=1, replica_groups=mesh['ctx'=128,'head'=2] {'head'}, dimensions={0} | all-to-all | bytes 1310720 | tf_op jit(solution)/shard_map/all_to_all | solution.py:175
  (641 shorter events, 252.0 us)
Async XLA Ops:
  0.0 0.8 copy-start
  2.2 7.3 copy-start.3
  219.6 12.2 %copy-start.2 = (bf16[256,256]{1,0:T(8,128)(2,1)S(1)}, bf16[256,256]{1,0:T(8,128)(2,1)}, u32[]{:S(2)}) copy-start(bf16[256,256]{1,0:T(8,128)(2,1)} %param.19) | copy-start | bytes 393220
  219.6 192.3 %all-to-all-start.1 = ((bf16[128,128,256]{2,1,0:T(8,128)(2,1)}), bf16[128,128,256]{2,1,0:T(8,128)(2,1)}, u32[]{:S(2)}, u32[]{:S(2)}) async-start(bf16[128,128,256]{2,1,0:T(8,128)(2,1)} %get-tuple-element.1138), calls=%async_computation.1 | async-start | bytes 16777216 | tf_op jit(solution)/shard_map/all_to_all | solution.py:154
  239.1 180.1 %copy-start.4 = (s32[2,16]{1,0:T(2,128)S(1)}, s32[2,16]{1,0:T(2,128)}, u32[]{:S(2)}) copy-start(s32[2,16]{1,0:T(2,128)} %param.21) | copy-start | bytes 388
  239.1 180.1 %copy-start.5 = (s32[2]{0:T(128)S(1)}, s32[2]{0:T(128)}, u32[]{:S(2)}) copy-start(s32[2]{0:T(128)} %param.22) | copy-start | bytes 28
  797.5 11.1 %copy-start.1 = (s32[64,128]{1,0:T(8,128)S(1)}, s32[64,128]{1,0:T(8,128)}, u32[]{:S(2)}) copy-start(s32[64,128]{1,0:T(8,128)} %param.23) | copy-start | bytes 98308
where the time goes:
time: 812 us; the launch traced here: 809 us
  local copies, waits for them, and re-layouts  267 us (33%)
  blocking collectives  204 us (25%)
  waiting for transfers between devices  173 us (21%)
  other arithmetic  95.2 us (12%)
  matrix products  39.6 us (5%)
  loops' own time  18.1 us (2%)
  starting transfers between devices  12.1 us (1%)
    all_to_all x1, blocking collectives, on_device(): lax.all_to_all(jnp.take(key_blocks, chosen, axis=0), 'ctx', split_axis=0,...  194 us
    all_to_all x1, waiting for transfers between devices, on_device(): lax.all_to_all(jnp.take(value_blocks, chosen, axis=0), 'ctx', split_axis=...  173 us
    gather x40, local copies, waits for them, and re-layouts, tile_rows(): selected_blocks = jnp.take(pool, tile_ids, axis=0)  159 us
    dynamic_slice x40, local copies, waits for them, and re-layouts, second_pass(): lax.dynamic_index_in_dim(stored_scores, step_index, 0, keepdims=False)  36.2 us
    dot_general x20, matrix products, first_pass(): jnp.einsum('gqd,kd->gqk', query_head, keys_now, preferred_element_type=jn...  28.6 us
    gather x40, local copies, waits for them, and re-layouts, tile_list(): owners[far_slot]  25.6 us
    and x40, other arithmetic, tile_rows(): selected_blocks = jnp.take(pool, tile_ids, axis=0)  25.5 us
    select_n x40, other arithmetic, tile_list(): owners[far_slot]  25.5 us
  transfers between devices with their start and end apart: 1, of which 1 were waited for; matrix products, arithmetic and copies ran while one was open for 1% of the time, Pallas kernels for 0%

commit v1 on v0

v1 whole, which is shorter than its diff:
```python
import functools

import jax
import jax.numpy as jnp
from jax import lax
from jax.experimental import pallas as pl
from jax.experimental.pallas import tpu as pltpu
from jax.sharding import Mesh, PartitionSpec as P

HEAD_WIDTH = 128
BLOCK_TOKENS = 128
GROUP = 5
QCOLS = GROUP * HEAD_WIDTH
NY, NZ, NX = 4, 8, 4
SHARDS = NY * NZ * NX
FMAX = 16
SLOTS = 32
ITEMS = 16
LIST = 20
STEP = 4
NEG = -1e30
EXP_SCALE = 1.4426950408889634 * HEAD_WIDTH ** (-0.5)


def attend_kernel(
    meta_ref, q_ref, kv_ref, o_ref, lse_ref,
    list_ref, count_ref, acc_ref, m_ref, l_ref,
):
    y, z, x = (lax.axis_index(a) for a in ("y", "z", "x"))

    def place(item):
        pattern, target, row = item >> 3, (item >> 1) & 3, item & 1
        along_x = pattern == 0
        own = jnp.where(along_x, target == x, target == y)
        own_slot = z * 4 + jnp.where(along_x, y, x)
        return pattern, target, row, along_x, own, own_slot

    def build(item, carry):
        pattern, target, row, along_x, own, own_slot = place(item)
        base = (item >> 1) * 1024 + row * 128
        at = item * LIST
        list_ref[at] = own_slot * 2
        n = jnp.logical_and(own, row == 1).astype(jnp.int32)
        for j in range(FMAX):
            code = meta_ref[base + j]
            oy, oz, ox = code >> 6, (code >> 3) & 7, (code >> 1) & 3
            list_ref[at + n] = oz * 8 + jnp.where(along_x, oy, ox) * 2 + (code & 1)
            mine = jnp.logical_and(code >= 0, jnp.where(along_x, ox == x, oy == y))
            n = n + mine.astype(jnp.int32)
        count_ref[item] = n
        return carry

    lax.fori_loop(0, ITEMS, build, 0)

    def one_item(item, carry):
        pattern, target, row, along_x, own, own_slot = place(item)

        total = count_ref[item]
        at = item * LIST
        tokens = pl.ds(pl.multiple_of(row * BLOCK_TOKENS, BLOCK_TOKENS), BLOCK_TOKENS)
        q = q_ref.at[pattern, target, tokens]
        acc_ref[...] = jnp.zeros_like(acc_ref)
        m_ref[...] = jnp.full_like(m_ref, NEG)
        l_ref[...] = jnp.zeros_like(l_ref)

        def rows_of(kind, blocks):
            starts = [pl.multiple_of((2 * kind + (b & 1)) * BLOCK_TOKENS, BLOCK_TOKENS) for b in blocks]
            return jnp.concatenate(
                [kv_ref[pattern, b >> 1, pl.ds(i, BLOCK_TOKENS)] for b, i in zip(blocks, starts)], 0
            )

        def absorb(blocks, masked):
            parts = [slice(i * BLOCK_TOKENS, (i + 1) * BLOCK_TOKENS) for i in range(len(blocks))]
            heads = jnp.concatenate(
                [q[:, g * HEAD_WIDTH : (g + 1) * HEAD_WIDTH] for g in range(GROUP)], 0
            )
            s = lax.dot_general(
                heads, rows_of(0, blocks), (((1,), (1,)), ((), ())),
                preferred_element_type=jnp.float32,
            )
            if masked:
                query_pos = lax.broadcasted_iota(jnp.int32, s.shape, 0) & (BLOCK_TOKENS - 1)
                key_pos = lax.broadcasted_iota(jnp.int32, s.shape, 1)
                s = jnp.where(key_pos <= query_pos, s, NEG)
            m_old = m_ref[...]
            top = functools.reduce(jnp.maximum, [s[:, c] for c in parts])
            m_new = jnp.maximum(m_old, jnp.max(top, axis=1, keepdims=True))
            alpha = jnp.exp2((m_old - m_new) * EXP_SCALE)
            p = [jnp.exp2((s[:, c] - m_new) * EXP_SCALE) for c in parts]
            m_ref[...] = m_new
            gained = jnp.sum(functools.reduce(jnp.add, p), axis=1, keepdims=True)
            l_ref[...] = l_ref[...] * alpha + gained
            acc_ref[...] = acc_ref[...] * alpha + jnp.dot(
                jnp.concatenate(p, 1).astype(jnp.bfloat16), rows_of(1, blocks),
                preferred_element_type=jnp.float32,
            )

        @pl.when(own)
        def _():
            absorb([own_slot * 2 + row], True)

        def many(i, carry):
            absorb([list_ref[at + STEP * i + k] for k in range(STEP)], False)
            return carry

        lax.fori_loop(0, total // STEP, many, 0)
        done = total - total % STEP
        for k in (2, 1):

            @pl.when((total & k) != 0)
            def _(k=k, done=done):
                absorb([list_ref[at + done + i] for i in range(k)], False)

            done = done + (total & k)

        lane = lax.broadcasted_iota(jnp.int32, (BLOCK_TOKENS, BLOCK_TOKENS), 1)
        tile = jnp.zeros((BLOCK_TOKENS, BLOCK_TOKENS), jnp.float32)
        for g in range(GROUP):
            part = slice(g * HEAD_WIDTH, (g + 1) * HEAD_WIDTH)
            l = l_ref[part]
            live = l > 0
            safe = jnp.where(live, l, 1.0)
            o_ref[item, :, part] = (acc_ref[part] * (1.0 / safe)).astype(jnp.bfloat16)
            lse = jnp.where(live, m_ref[part] * EXP_SCALE + jnp.log2(safe), NEG)
            tile = jnp.where(lane == g, lse, tile)
        lse_ref[item] = tile.T[:8]
        return carry

    lax.fori_loop(0, ITEMS, one_item, 0)


def attend(meta, q, kv):
    blocks = pl.BlockSpec(memory_space=pltpu.VMEM)
    scalars = pl.BlockSpec(memory_space=pltpu.SMEM)
    state = pltpu.VMEM((QCOLS, HEAD_WIDTH), jnp.float32)
    return pl.pallas_call(
        attend_kernel,
        in_specs=[scalars, blocks, blocks],
        out_specs=[blocks, blocks],
        out_shape=[
            jax.ShapeDtypeStruct((ITEMS, BLOCK_TOKENS, QCOLS), jnp.bfloat16),
            jax.ShapeDtypeStruct((ITEMS, 8, BLOCK_TOKENS), jnp.float32),
        ],
        scratch_shapes=[
            pltpu.SMEM((ITEMS * LIST,), jnp.int32),
            pltpu.SMEM((ITEMS,), jnp.int32),
            state, state, state,
        ],
        compiler_params=pltpu.CompilerParams(vmem_limit_bytes=32 * 1024 * 1024),
    )(meta, q, kv)


def return_kernel(o_in, lse_in, out_ref, o_got, lse_got, send, recv, lse_send, lse_recv):
    at = {"x": lax.axis_index("x"), "y": lax.axis_index("y")}
    core = lax.axis_index("head")
    axes = ("x", "y")
    others = [(p, step, e) for step in (1, 3, 2, 0) for e in range(2) for p in range(2)]
    others = [v for v in others if v[1:] != (0, 0)]

    def device(p, step, e):
        a = axes[p]
        return {a: (at[a] + step) % 4, "head": (core + e) % 2}

    barrier = pltpu.get_barrier_semaphore()
    met = [v for v in others if v != (1, 0, 1)]
    for v in met:
        pl.semaphore_signal(
            barrier, inc=1, device_id=device(*v), device_id_type=pl.DeviceIdType.MESH
        )
    pl.semaphore_wait(barrier, len(met))

    def copies(p, step, e):
        a = axes[p]
        target, row = (at[a] + step) % 4, (core + e) % 2
        i = (p * 4 + step) * 2 + e
        parts = (
            (o_in.at[(p * 4 + target) * 2 + row], o_got.at[p, core, at[a]], send, recv),
            (lse_in.at[(p * 4 + target) * 2 + row], lse_got.at[p, core, at[a]], lse_send, lse_recv),
        )
        if step == 0 and e == 0:
            return [pltpu.make_async_copy(s, d, r.at[i]) for s, d, _, r in parts]
        return [
            pltpu.make_async_remote_copy(
                src_ref=s, dst_ref=d, send_sem=w.at[i], recv_sem=r.at[i],
                device_id=device(p, step, e), device_id_type=pl.DeviceIdType.MESH,
            )
            for s, d, w, r in parts
        ]

    for v in others + [(0, 0, 0), (1, 0, 0)]:
        for c in copies(*v):
            c.start()
    for p in range(2):
        for e in range(2):
            for step in range(4):
                for c in copies(p, step, e):
                    if (step, e) == (0, 0):
                        c.wait()
                    else:
                        c.wait_recv()
    for p in range(2):
        for c in range(2):
            lse = [lse_got[p, c, i] for i in range(4)]
            top = functools.reduce(jnp.maximum, lse)
            w = [jnp.exp2(v - top) for v in lse]
            inv = 1.0 / functools.reduce(jnp.add, w)
            w = [v * inv for v in w]
            rest = jnp.zeros((BLOCK_TOKENS - 32, BLOCK_TOKENS), jnp.float32)
            w = jnp.concatenate(w + [rest], 0).T
            for g in range(GROUP):
                cols = slice(g * HEAD_WIDTH, (g + 1) * HEAD_WIDTH)
                mixed = sum(
                    o_got[p, c, i, :, cols].astype(jnp.float32) * w[:, i * 8 + g : i * 8 + g + 1]
                    for i in range(4)
                )
                start = (c * 2 + p) * QCOLS + g * HEAD_WIDTH
                out_ref[:, start : start + HEAD_WIDTH] = mixed.astype(jnp.bfloat16)
    for v in others:
        for c in copies(*v):
            c.wait_send()


def send_back(o, lse):
    dma = pltpu.SemaphoreType.DMA
    any_spec = pl.BlockSpec(memory_space=pl.ANY)
    return pl.pallas_call(
        return_kernel,
        in_specs=[any_spec] * 2,
        out_specs=pl.BlockSpec(memory_space=pltpu.VMEM),
        out_shape=jax.ShapeDtypeStruct((BLOCK_TOKENS, 4 * QCOLS), jnp.bfloat16),
        scratch_shapes=[
            pltpu.VMEM((2, 2, 4, BLOCK_TOKENS, QCOLS), jnp.bfloat16),
            pltpu.VMEM((2, 2, 4, 8, BLOCK_TOKENS), jnp.float32),
            dma((16,)), dma((16,)), dma((16,)), dma((16,)),
        ],
        compiler_params=pltpu.CompilerParams(
            collective_id=1, has_side_effects=True, vmem_limit_bytes=16 * 1024 * 1024
        ),
    )(o, lse)


def copy_to(src, dst, sems, device):
    return pltpu.make_async_remote_copy(
        src_ref=src, dst_ref=dst, send_sem=sems[0], recv_sem=sems[1],
        device_id=device, device_id_type=pl.DeviceIdType.MESH,
    )


MAIN = 3 * BLOCK_TOKENS
LAST = BLOCK_TOKENS
ORDER = (
    ("last near", 0, 0), ("last near", 0, 1), ("z", 1, 0), ("near", 0, 0), ("near", 0, 1),
    ("z", 1, 1), ("z", 2, 0), ("z", 2, 1), ("q", 0, 1), ("q", 0, 0), ("last far", 0, 0),
    ("z", 3, 0), ("last far", 0, 1), ("near", 1, 0), ("z", 3, 1), ("near", 1, 1), ("near", 2, 0),
    ("last z", 1, 0), ("near", 2, 1), ("z", 4, 0), ("near", 3, 0), ("near", 3, 1),
    ("last z", 1, 1), ("near", 4, 0), ("near", 4, 1), ("z", 4, 1), ("last z", 2, 0),
    ("near", 5, 0), ("near", 5, 1), ("last z", 2, 1), ("near", 6, 0), ("near", 6, 1),
    ("last z", 3, 0), ("last z", 3, 1), ("near", 7, 0), ("last z", 4, 0), ("near", 7, 1),
    ("last z", 4, 1),
)


def gather_kernel(
    q_hbm, k_hbm, v_hbm, owners_hbm, pairs_hbm, counts_in, q_all, kv_all, meta_all,
    q_in, k_in, v_in, owners_in, pairs_in, q_own, kv_own, meta_own, in_sem, local_sem,
    z_send, z_recv, near_send, near_recv, far_send, far_recv,
    lz_send, lz_recv, ln_send, ln_recv, lf_send, lf_recv,
    q_send, q_recv, qf_send, qf_recv, t_send, t_recv,
):
    at = {a: lax.axis_index(a) for a in ("y", "z", "x")}
    size = {"y": NY, "z": NZ, "x": NX}
    ring = {a: ((at[a] + 1) % size[a], (at[a] + size[a] - 1) % size[a]) for a in at}

    barrier = pltpu.get_barrier_semaphore()
    for a in at:
        for n in ring[a]:
            pl.semaphore_signal(
                barrier, inc=1, device_id={a: n}, device_id_type=pl.DeviceIdType.MESH
            )

    loads = [
        pltpu.make_async_copy(src, dst, in_sem.at[i])
        for i, (src, dst) in enumerate(
            (
                (k_hbm, k_in), (v_hbm, v_in), (q_hbm, q_in),
                (owners_hbm, owners_in), (pairs_hbm, pairs_in),
            )
        )
    ]
    for c in loads:
        c.start()

    side = ("y", "x")
    cross = ("x", "y")

    def slot(h, place, zo):
        return zo * 4 + place

    local = []

    def keep(src, dst):
        c = pltpu.make_async_copy(src, dst, local_sem.at[len(local)])
        c.start()
        local.append(c)

    sends = []

    def part(d):
        return pl.ds(d * (MAIN // 2), MAIN // 2)

    def z_copy(d, s, h):
        back = at["z"] - (s - 1) if d == 0 else at["z"] + (s - 1)
        rows = part(d) if s == 4 else pl.ds(0, MAIN)
        ref = kv_all.at[h, slot(h, at[side[h]], (back + NZ) % NZ), rows]
        i = (d * 4 + s - 1) * 2 + h
        src = kv_own.at[h, rows] if s == 1 else ref
        return copy_to(src, ref, (z_send.at[i], z_recv.at[i]), {"z": ring["z"][d]})

    def near_copy(h, i, zo, d):
        rows = pl.ds(0, MAIN)
        ref = kv_all.at[h, slot(h, at[side[h]], zo), rows]
        n = (h * 8 + i) * 2 + d
        src = kv_own.at[h, rows] if i == 0 else ref
        return copy_to(src, ref, (near_send.at[n], near_recv.at[n]), {side[h]: ring[side[h]][d]})

    def far_copy(h, i, zo, d):
        a = side[h]
        ref = kv_all.at[h, slot(h, ring[a][1 - d], zo), part(d)]
        n = (h * 8 + i) * 2 + d
        return copy_to(ref, ref, (far_send.at[n], far_recv.at[n]), {a: ring[a][d]})

    def last_near(h, d):
        a = side[h]
        rows = pl.ds(MAIN, LAST)
        ref = kv_all.at[h, slot(h, at[a], at["z"]), rows]
        n = h * 2 + d
        return copy_to(kv_own.at[h, rows], ref, (ln_send.at[n], ln_recv.at[n]), {a: ring[a][d]})

    def last_far(h, d):
        a = side[h]
        rows = pl.ds(MAIN + d * (LAST // 2), LAST // 2)
        ref = kv_all.at[h, slot(h, ring[a][1 - d], at["z"]), rows]
        n = h * 2 + d
        return copy_to(ref, ref, (lf_send.at[n], lf_recv.at[n]), {a: ring[a][d]})

    def last_z(d, s, h):
        back = at["z"] - (s - 1) if d == 0 else at["z"] + (s - 1)
        first = ((back + NZ) % NZ) * 4
        places = pl.ds(first + 2 * d, 2) if s == 4 else pl.ds(first, 4)
        ref = kv_all.at[h, places, pl.ds(MAIN, LAST)]
        i = (d * 4 + s - 1) * 2 + h
        return copy_to(ref, ref, (lz_send.at[i], lz_recv.at[i]), {"z": ring["z"][d]})

    def q_copy(h, d):
        a = cross[h]
        ref = q_all.at[h, at[a]]
        return copy_to(
            q_own.at[h], ref, (q_send.at[h * 2 + d], q_recv.at[h * 2 + d]), {a: ring[a][d]}
        )

    def qf_copy(h, d):
        a = cross[h]
        ref = q_all.at[h, ring[a][1 - d], pl.ds(d * BLOCK_TOKENS, BLOCK_TOKENS)]
        return copy_to(
            ref, ref, (qf_send.at[h * 2 + d], qf_recv.at[h * 2 + d]), {a: ring[a][d]}
        )

    def t_copy(h, d, relay):
        a = cross[h]
        ref = meta_all.at[h, ring[a][1 - d] if relay else at[a]]
        i = (h * 2 + d) * 2 + relay
        return copy_to(
            ref if relay else meta_own, ref, (t_send.at[i], t_recv.at[i]), {a: ring[a][d]}
        )

    def start(c):
        c.start()
        sends.append(c)

    both = [(h, d) for h in range(2) for d in range(2)]
    zs = [at["z"]]
    for s in range(1, 5):
        zs.append((at["z"] - s + NZ) % NZ)
        zs.append((at["z"] + s) % NZ)
    zs = zs[:8]

    for i, ref in enumerate((k_in, v_in)):
        loads[i].wait()
        for h in range(2):
            kv_own[h, i * 256 : i * 256 + 256] = ref[:, h * HEAD_WIDTH : (h + 1) * HEAD_WIDTH]
    pl.semaphore_wait(barrier, 6)
    for h, d in both:
        start(z_copy(d, 1, h))
    for h, d in both:
        start(last_near(h, d))
    for h, d in both:
        start(near_copy(h, 0, zs[0], d))
    for h in range(2):
        keep(kv_own.at[h], kv_all.at[h, slot(h, at[side[h]], at["z"])])
    loads[2].wait()
    for h in range(2):
        q_own[h] = q_in[:, h * QCOLS : (h + 1) * QCOLS]
    for h, d in both:
        start(q_copy(h, d))

    for c in loads[3:]:
        c.wait()
    meta_own[...] = jnp.zeros_like(meta_own)
    meta_own[0:2, 0:FMAX] = owners_in[...]
    owners = meta_own[...]
    shard = (at["y"] * NZ + at["z"]) * NX + at["x"]
    listed = pairs_in[pl.ds(jnp.minimum(shard, SHARDS - 1 - shard), 1), :]
    half = jnp.take_along_axis(jnp.broadcast_to(listed, (8, 128)), owners, axis=1) & 1
    row = lax.broadcasted_iota(jnp.int32, (8, 128), 0)
    lane = lax.broadcasted_iota(jnp.int32, (8, 128), 1)
    count = jnp.where(row == 0, counts_in[0], jnp.where(row == 1, counts_in[1], 0))
    meta_own[...] = jnp.where(lane < count, owners * 2 + half, -1)
    for h, d in both:
        start(t_copy(h, d, 0))
    for h in range(2):
        keep(q_own.at[h], q_all.at[h, at[cross[h]]])
        keep(meta_own, meta_all.at[h, at[cross[h]]])

    def arrived(kind, i, h):
        for d in range(2):
            if kind == "z":
                z_copy(d, i, h).wait_recv()
                if i < 4:
                    start(z_copy(d, i + 1, h))
                    for e in range(2):
                        start(near_copy(h, 2 * i - 1 + d, zs[2 * i - 1 + d], e))
                elif d == 1:
                    for e in range(2):
                        start(near_copy(h, 7, zs[7], e))
            elif kind == "near":
                near_copy(h, i, zs[i], d).wait_recv()
                start(far_copy(h, i, zs[i], d))
            elif kind == "q":
                q_copy(h, d).wait_recv()
                start(qf_copy(h, d))
            elif kind == "last near":
                last_near(h, d).wait_recv()
                start(last_far(h, d))
            elif kind == "last far":
                last_far(h, d).wait_recv()
                if d == 1:
                    local[h].wait()
                    for e in range(2):
                        start(last_z(e, 1, h))
            else:
                last_z(d, i, h).wait_recv()
                if i < 4:
                    start(last_z(d, i + 1, h))

    for event in ORDER:
        arrived(*event)
    for h in range(2):
        for d in range(2):
            t_copy(h, d, 0).wait_recv()
        start(t_copy(h, 0, 1))
    for h, d in both:
        qf_copy(h, d).wait_recv()
        for i in range(8):
            far_copy(h, i, zs[i], d).wait_recv()
    for h in range(2):
        t_copy(h, 0, 1).wait_recv()
    for c in sends:
        c.wait_send()
    for c in local[2:]:
        c.wait()


def gather_all(q, k, v, owners, counts, pairs):
    dma = pltpu.SemaphoreType.DMA
    any_spec = pl.BlockSpec(memory_space=pl.ANY)
    arrays = [pltpu.with_memory_space_constraint(a, pltpu.HBM) for a in (q, k, v, owners, pairs)]
    return pl.pallas_call(
        gather_kernel,
        in_specs=[any_spec] * 5 + [pl.BlockSpec(memory_space=pltpu.SMEM)],
        out_specs=[any_spec] * 3,
        out_shape=[
            jax.ShapeDtypeStruct((2, 4, 2 * BLOCK_TOKENS, QCOLS), jnp.bfloat16),
            jax.ShapeDtypeStruct((2, SLOTS, MAIN + LAST, HEAD_WIDTH), jnp.bfloat16),
            jax.ShapeDtypeStruct((2, 4, 8, 128), jnp.int32),
        ],
        scratch_shapes=[pltpu.VMEM(a.shape, a.dtype) for a in (q, k, v, owners, pairs)]
        + [
            pltpu.VMEM((2, 2 * BLOCK_TOKENS, QCOLS), jnp.bfloat16),
            pltpu.VMEM((2, MAIN + LAST, HEAD_WIDTH), jnp.bfloat16),
            pltpu.VMEM((8, 128), jnp.int32),
        ]
        + [dma((n,)) for n in (5, 6, 16, 16, 32, 32, 32, 32, 16, 16, 4, 4, 4, 4, 4, 4, 4, 4, 8, 8)],
        compiler_params=pltpu.CompilerParams(
            collective_id=0, has_side_effects=True, vmem_limit_bytes=16 * 1024 * 1024
        ),
    )(*arrays, counts)


def on_device(queries, keys, values, far_owners, far_counts, pair_blocks):
    q, kv, meta = gather_all(queries, keys, values, far_owners, far_counts, pair_blocks)
    o, lse = attend(meta.reshape(-1), q, kv)
    return send_back(o, lse)


def solution(mesh):
    grid = Mesh(mesh.devices.reshape(NY, NZ, NX, 2), ("y", "z", "x", "head"))
    ctx = ("y", "z", "x")
    placed = (P(ctx, "head"), P(ctx, "head"), P(ctx, "head"), P(ctx, None), P(ctx), P())
    return jax.shard_map(
        on_device,
        mesh=grid,
        in_specs=placed,
        out_specs=P((*ctx, "head"), None),
        check_vma=False,
    )
```

time: 812 us -> 100 us (0.12)
  the two profiles are of different devices: /device:TPU:249 before, /device:TPU:65 now
where the time goes in v1:
time: 100 us
  Pallas kernels  98.9 us (99%)
  local copies, waits for them, and re-layouts  1.49 us (1%)
    pallas_call x1, Pallas kernels, gather_all(): pl.pallas_call(gather_kernel, in_specs=[any_spec] * 5 + [pl.BlockSpec(mem...  47 us
    pallas_call x1, Pallas kernels, attend(): pl.pallas_call(attend_kernel, in_specs=[scalars, blocks, blocks], out_spe...  26.5 us
    pallas_call x1, Pallas kernels, send_back(): pl.pallas_call(return_kernel, in_specs=[any_spec] * 2, out_specs=pl.Block...  25.4 us

profile of v1, /device:TPU:65, one launch (start us, length us, event | category | flops | bytes accessed | tf_op | source)
XLA Modules:
  0.0 100.4 jit_solution(15370177717906539511)
XLA Ops:
  0.0 0.0 copy-start
  0.0 0.7 copy-done
  0.7 47.0 %shard_map.64 = (bf16[2,4,256,640]{3,2,1,0:T(8,128)(2,1)S(1)}, bf16[2,32,512,128]{3,2,1,0:T(8,128)(2,1)S(1)}, s32[2,4,8,128]{3,2,1,0:T(8,128)S(1)}) custom-call(bf16[256,1280]{1,0:T(8,128)(2,1)} %q_hbm.1, bf16[256,256]{1,0:T(8,128)(2,1)} %k_hbm.1, bf16[256,256]{1,0:T(8,128)(2,1)} %v_hbm.1, s32[2,16]{1,0:T(2,128)} %owners_hbm.1, s32[64,128]{1,0:T(8,128)} %pairs_hbm.1, ...), custom_call_target="tpu_custom_call" | custom-call | tf_op jit(solution)/shard_map/pallas_call | solution.py:477
  47.7 26.5 %shard_map.65 = (bf16[16,128,640]{2,1,0:T(8,128)(2,1)S(1)}, f32[16,8,128]{2,1,0:T(8,128)S(1)}) custom-call(s32[8192]{0:T(1024)S(1)} %bitcast.1, bf16[2,4,256,640]{3,2,1,0:T(8,128)(2,1)S(1)} %get-tuple-element.11.q_ref, bf16[2,32,512,128]{3,2,1,0:T(8,128)(2,1)S(1)} %get-tuple-element.12.kv_ref), custom_call_target="tpu_custom_call" | custom-call | tf_op jit(solution)/shard_map/pallas_call | solution.py:136
  74.2 25.4 %shard_map.66 = bf16[128,2560]{1,0:T(8,128)(2,1)S(1)} custom-call(bf16[16,128,640]{2,1,0:T(8,128)(2,1)S(1)} %get-tuple-element.13.o_in, f32[16,8,128]{2,1,0:T(8,128)S(1)} %get-tuple-element.14.lse_in), custom_call_target="tpu_custom_call" | custom-call | tf_op jit(solution)/shard_map/pallas_call | solution.py:226
  99.5 0.8 copy.8
Async XLA Ops:
  0.0 0.7 copy-start

commit v2 on v1

--- a/solution.py
+++ b/solution.py
@@ -16,141 +16,189 @@
 FMAX = 16
 SLOTS = 32
 ITEMS = 16
-LIST = 20
-STEP = 4
+STEP = 2
+UNROLL = 4
 NEG = -1e30
 EXP_SCALE = 1.4426950408889634 * HEAD_WIDTH ** (-0.5)
 
 
 def attend_kernel(
-    meta_ref, q_ref, kv_ref, o_ref, lse_ref,
-    list_ref, count_ref, acc_ref, m_ref, l_ref,
+    codes_ref, q_in, kv_in, o_ref, stat_ref,
+    count_ref, chunk_ref, q_ref, kv_ref, acc_ref, m_ref, l_ref, sem,
 ):
     y, z, x = (lax.axis_index(a) for a in ("y", "z", "x"))
 
-    def place(item):
-        pattern, target, row = item >> 3, (item >> 1) & 3, item & 1
-        along_x = pattern == 0
-        own = jnp.where(along_x, target == x, target == y)
-        own_slot = z * 4 + jnp.where(along_x, y, x)
-        return pattern, target, row, along_x, own, own_slot
-
-    def build(item, carry):
-        pattern, target, row, along_x, own, own_slot = place(item)
-        base = (item >> 1) * 1024 + row * 128
-        at = item * LIST
-        list_ref[at] = own_slot * 2
-        n = jnp.logical_and(own, row == 1).astype(jnp.int32)
-        for j in range(FMAX):
-            code = meta_ref[base + j]
-            oy, oz, ox = code >> 6, (code >> 3) & 7, (code >> 1) & 3
-            list_ref[at + n] = oz * 8 + jnp.where(along_x, oy, ox) * 2 + (code & 1)
-            mine = jnp.logical_and(code >= 0, jnp.where(along_x, ox == x, oy == y))
-            n = n + mine.astype(jnp.int32)
+    def loads(pattern):
+        return [
+            pltpu.make_async_copy(src.at[pattern], dst.at[pattern], sem.at[i, pattern])
+            for i, (src, dst) in enumerate(((q_in, q_ref), (kv_in, kv_ref)))
+        ]
+
+    for c in loads(0) + loads(1):
+        c.start()
+
+    def base_of(pattern, item):
+        return (item >> 1) * 1024 + (item & 1) * 128 + (x if pattern == 0 else y) * FMAX
+
+    def build(pattern, item, chunks):
+        n = codes_ref[base_of(pattern, item) + 2 * 128]
         count_ref[item] = n
+
+        def note(i, chunks):
+            chunk_ref[chunks] = item * 16 + i
+            return chunks + 1
+
+        return lax.fori_loop(0, (n + STEP - 1) // STEP, note, chunks)
+
+    middle = lax.fori_loop(0, 8, functools.partial(build, 0), jnp.int32(0))
+    end = lax.fori_loop(8, 16, functools.partial(build, 1), middle)
+
+    def score(pattern, item, blocks):
+        tokens = pl.ds(pl.multiple_of((item & 1) * BLOCK_TOKENS, BLOCK_TOKENS), BLOCK_TOKENS)
+        q = q_ref.at[pattern, (item >> 1) & 3, tokens]
+        heads = [q[:, g * HEAD_WIDTH : (g + 1) * HEAD_WIDTH] for g in range(GROUP)]
+        return lax.dot_general(
+            jnp.concatenate(heads, 0), rows_of(pattern, 0, blocks), (((1,), (1,)), ((), ())),
+            preferred_element_type=jnp.float32,
+        )
+
+    def rows_of(pattern, kind, blocks):
+        starts = [
+            pl.multiple_of((2 * kind + (b & 1)) * BLOCK_TOKENS, BLOCK_TOKENS) for b in blocks
+        ]
+        return jnp.concatenate(
+            [kv_ref[pattern, b >> 1, pl.ds(i, BLOCK_TOKENS)] for b, i in zip(blocks, starts)], 0
+        )
+
+    def split(s):
+        return [
+            s[:, i : i + BLOCK_TOKENS] for i in range(0, s.shape[1], BLOCK_TOKENS)
+        ]
+
+    def top_of(parts):
+        return jnp.max(functools.reduce(jnp.maximum, parts), axis=1, keepdims=True)
+
+    def mix(pattern, blocks, p):
+        return jnp.dot(
+            jnp.concatenate(p, 1).astype(jnp.bfloat16), rows_of(pattern, 1, blocks),
+            preferred_element_type=jnp.float32,
+        )
+
+    def own_blocks(pattern, row):
+        place = y if pattern == 0 else x
+        item = (pattern * 4 + (x if pattern == 0 else y)) * 2 + row
+        blocks = [(z * 4 + place) * 2 + i for i in range(row + 1)]
+        parts = split(score(pattern, item, blocks))
+        query_pos = lax.broadcasted_iota(jnp.int32, parts[0].shape, 0) & (BLOCK_TOKENS - 1)
+        key_pos = lax.broadcasted_iota(jnp.int32, parts[0].shape, 1)
+        parts[-1] = jnp.where(key_pos <= query_pos, parts[-1], NEG)
+        m = top_of(parts)
+        p = [jnp.exp2((v - m) * EXP_SCALE) for v in parts]
+        m_ref[item] = jnp.broadcast_to(m, (QCOLS, HEAD_WIDTH))
+        l_ref[item] = functools.reduce(jnp.add, p)
+        acc_ref[item] = mix(pattern, blocks, p)
+
+    def fetch(pattern, c):
+        code = chunk_ref[c]
+        item, i = code >> 4, code & 15
+        at = base_of(pattern, item) + i * STEP
+        blocks = [codes_ref[at + k] for k in range(STEP)]
+        own = ((item >> 1) & 3) == (x if pattern == 0 else y)
+        fresh = jnp.logical_and(i == 0, jnp.logical_not(own))
+        return item, blocks, count_ref[item] - i * STEP, fresh
+
+    def absorb(pattern, s, item, blocks, left, fresh):
+        parts = split(s)
+        m_old = jnp.where(fresh, NEG, m_ref[item])
+        m_new = jnp.maximum(m_old, top_of(parts))
+        alpha = jnp.exp2((m_old - m_new) * EXP_SCALE)
+        off = m_new * EXP_SCALE
+        p = [
+            jnp.exp2(v * EXP_SCALE - (off if i == 0 else off + jnp.where(left > i, 0.0, -NEG)))
+            for i, v in enumerate(parts)
+        ]
+        m_ref[item] = m_new
+        l_ref[item] = jnp.where(fresh, 0.0, l_ref[item]) * alpha + functools.reduce(jnp.add, p)
+        acc_ref[item] = jnp.where(fresh, 0.0, acc_ref[item]) * alpha + mix(pattern, blocks, p)
+
+    for pattern, begin, stop in ((0, 0, middle), (1, middle, end)):
+        for c in loads(pattern):
+            c.wait()
+        for row in range(2):
+            own_blocks(pattern, row)
+
+        def several(j, carry, pattern=pattern, begin=begin):
+            got = [fetch(pattern, begin + j * UNROLL + u) for u in range(UNROLL)]
+            scores = [score(pattern, g[0], g[1]) for g in got]
+            for g, s in zip(got, scores):
+                absorb(pattern, s, *g)
+            return carry
+
+        def single(c, carry, pattern=pattern):
+            g = fetch(pattern, c)
+            absorb(pattern, score(pattern, g[0], g[1]), *g)
+            return carry
+
+        whole = (stop - begin) // UNROLL
+        lax.fori_loop(0, whole, several, 0)
+        lax.fori_loop(begin + whole * UNROLL, stop, single, 0)
+
+    lane = lax.broadcasted_iota(jnp.int32, (BLOCK_TOKENS, BLOCK_TOKENS), 1)
+
+    def close(item, carry):
+        own = ((item >> 1) & 3) == jnp.where(item < 8, x, y)
+        read = jnp.logical_or(own, count_ref[item] > 0)
+
+        @pl.when(read)
+        def _():
+            tops = jnp.zeros((BLOCK_TOKENS, BLOCK_TOKENS), jnp.float32)
+            sums = jnp.zeros((BLOCK_TOKENS, BLOCK_TOKENS), jnp.float32)
+            for g in range(GROUP):
+                part = slice(g * HEAD_WIDTH, (g + 1) * HEAD_WIDTH)
+                o_ref[item, :, part] = acc_ref[item, part].astype(jnp.bfloat16)
+                tops = jnp.where(lane == g, m_ref[item, part], tops)
+                sums = jnp.where(
+                    lane == g, jnp.sum(l_ref[item, part], axis=1, keepdims=True), sums
+                )
+            stat_ref[item, 0:8] = tops.T[:8] * EXP_SCALE
+            stat_ref[item, 8:16] = sums.T[:8]
+
+        @pl.when(jnp.logical_not(read))
+        def _():
+            o_ref[item] = jnp.zeros((BLOCK_TOKENS, QCOLS), jnp.bfloat16)
+            stat_ref[item, 0:8] = jnp.full((8, BLOCK_TOKENS), NEG, jnp.float32)
+            stat_ref[item, 8:16] = jnp.zeros((8, BLOCK_TOKENS), jnp.float32)
+
         return carry
 
-    lax.fori_loop(0, ITEMS, build, 0)
-
-    def one_item(item, carry):
-        pattern, target, row, along_x, own, own_slot = place(item)
-
-        total = count_ref[item]
-        at = item * LIST
-        tokens = pl.ds(pl.multiple_of(row * BLOCK_TOKENS, BLOCK_TOKENS), BLOCK_TOKENS)
-        q = q_ref.at[pattern, target, tokens]
-        acc_ref[...] = jnp.zeros_like(acc_ref)
-        m_ref[...] = jnp.full_like(m_ref, NEG)
-        l_ref[...] = jnp.zeros_like(l_ref)
-
-        def rows_of(kind, blocks):
-            starts = [pl.multiple_of((2 * kind + (b & 1)) * BLOCK_TOKENS, BLOCK_TOKENS) for b in blocks]
-            return jnp.concatenate(
-                [kv_ref[pattern, b >> 1, pl.ds(i, BLOCK_TOKENS)] for b, i in zip(blocks, starts)], 0
-            )
-
-        def absorb(blocks, masked):
-            parts = [slice(i * BLOCK_TOKENS, (i + 1) * BLOCK_TOKENS) for i in range(len(blocks))]
-            heads = jnp.concatenate(
-                [q[:, g * HEAD_WIDTH : (g + 1) * HEAD_WIDTH] for g in range(GROUP)], 0
-            )
-            s = lax.dot_general(
-                heads, rows_of(0, blocks), (((1,), (1,)), ((), ())),
-                preferred_element_type=jnp.float32,
-            )
-            if masked:
-                query_pos = lax.broadcasted_iota(jnp.int32, s.shape, 0) & (BLOCK_TOKENS - 1)
-                key_pos = lax.broadcasted_iota(jnp.int32, s.shape, 1)
-                s = jnp.where(key_pos <= query_pos, s, NEG)
-            m_old = m_ref[...]
-            top = functools.reduce(jnp.maximum, [s[:, c] for c in parts])
-            m_new = jnp.maximum(m_old, jnp.max(top, axis=1, keepdims=True))
-            alpha = jnp.exp2((m_old - m_new) * EXP_SCALE)
-            p = [jnp.exp2((s[:, c] - m_new) * EXP_SCALE) for c in parts]
-            m_ref[...] = m_new
-            gained = jnp.sum(functools.reduce(jnp.add, p), axis=1, keepdims=True)
-            l_ref[...] = l_ref[...] * alpha + gained
-            acc_ref[...] = acc_ref[...] * alpha + jnp.dot(
-                jnp.concatenate(p, 1).astype(jnp.bfloat16), rows_of(1, blocks),
-                preferred_element_type=jnp.float32,
-            )
-
-        @pl.when(own)
-        def _():
-            absorb([own_slot * 2 + row], True)
-
-        def many(i, carry):
-            absorb([list_ref[at + STEP * i + k] for k in range(STEP)], False)
-            return carry
-
-        lax.fori_loop(0, total // STEP, many, 0)
-        done = total - total % STEP
-        for k in (2, 1):
-
-            @pl.when((total & k) != 0)
-            def _(k=k, done=done):
-                absorb([list_ref[at + done + i] for i in range(k)], False)
-
-            done = done + (total & k)
-
-        lane = lax.broadcasted_iota(jnp.int32, (BLOCK_TOKENS, BLOCK_TOKENS), 1)
-        tile = jnp.zeros((BLOCK_TOKENS, BLOCK_TOKENS), jnp.float32)
-        for g in range(GROUP):
-            part = slice(g * HEAD_WIDTH, (g + 1) * HEAD_WIDTH)
-            l = l_ref[part]
-            live = l > 0
-            safe = jnp.where(live, l, 1.0)
-            o_ref[item, :, part] = (acc_ref[part] * (1.0 / safe)).astype(jnp.bfloat16)
-            lse = jnp.where(live, m_ref[part] * EXP_SCALE + jnp.log2(safe), NEG)
-            tile = jnp.where(lane == g, lse, tile)
-        lse_ref[item] = tile.T[:8]
-        return carry
-
-    lax.fori_loop(0, ITEMS, one_item, 0)
-
-
-def attend(meta, q, kv):
+    lax.fori_loop(0, ITEMS, close, 0)
+
+
+def attend(codes, q, kv):
+    any_spec = pl.BlockSpec(memory_space=pl.ANY)
     blocks = pl.BlockSpec(memory_space=pltpu.VMEM)
-    scalars = pl.BlockSpec(memory_space=pltpu.SMEM)
-    state = pltpu.VMEM((QCOLS, HEAD_WIDTH), jnp.float32)
+    state = pltpu.VMEM((ITEMS, QCOLS, HEAD_WIDTH), jnp.float32)
     return pl.pallas_call(
         attend_kernel,
-        in_specs=[scalars, blocks, blocks],
+        in_specs=[pl.BlockSpec(memory_space=pltpu.SMEM), any_spec, any_spec],
         out_specs=[blocks, blocks],
         out_shape=[
             jax.ShapeDtypeStruct((ITEMS, BLOCK_TOKENS, QCOLS), jnp.bfloat16),
-            jax.ShapeDtypeStruct((ITEMS, 8, BLOCK_TOKENS), jnp.float32),
+            jax.ShapeDtypeStruct((ITEMS, 16, BLOCK_TOKENS), jnp.float32),
         ],
         scratch_shapes=[
-            pltpu.SMEM((ITEMS * LIST,), jnp.int32),
             pltpu.SMEM((ITEMS,), jnp.int32),
+            pltpu.SMEM((ITEMS * FMAX,), jnp.int32),
+            pltpu.VMEM(q.shape, q.dtype),
+            pltpu.VMEM(kv.shape, kv.dtype),
             state, state, state,
+            pltpu.SemaphoreType.DMA((2, 2)),
         ],
-        compiler_params=pltpu.CompilerParams(vmem_limit_bytes=32 * 1024 * 1024),
-    )(meta, q, kv)
-
-
-def return_kernel(o_in, lse_in, out_ref, o_got, lse_got, send, recv, lse_send, lse_recv):
+        compiler_params=pltpu.CompilerParams(vmem_limit_bytes=40 * 1024 * 1024),
+    )(codes, q, kv)
+
+
+def return_kernel(o_in, stat_in, out_ref, o_got, stat_got, send, recv, stat_send, stat_recv):
     at = {"x": lax.axis_index("x"), "y": lax.axis_index("y")}
     core = lax.axis_index("head")
     axes = ("x", "y")
@@ -175,7 +223,7 @@
         i = (p * 4 + step) * 2 + e
         parts = (
             (o_in.at[(p * 4 + target) * 2 + row], o_got.at[p, core, at[a]], send, recv),
-            (lse_in.at[(p * 4 + target) * 2 + row], lse_got.at[p, core, at[a]], lse_send, lse_recv),
+            (stat_in.at[(p * 4 + target) * 2 + row], stat_got.at[p, core, at[a]], stat_send, stat_recv),
         )
         if step == 0 and e == 0:
             return [pltpu.make_async_copy(s, d, r.at[i]) for s, d, _, r in parts]
@@ -200,10 +248,11 @@
                         c.wait_recv()
     for p in range(2):
         for c in range(2):
-            lse = [lse_got[p, c, i] for i in range(4)]
-            top = functools.reduce(jnp.maximum, lse)
-            w = [jnp.exp2(v - top) for v in lse]
-            inv = 1.0 / functools.reduce(jnp.add, w)
+            stats = [stat_got[p, c, i] for i in range(4)]
+            top = functools.reduce(jnp.maximum, [v[:8] for v in stats])
+            w = [jnp.exp2(v[:8] - top) for v in stats]
+            total = functools.reduce(jnp.add, [v[8:] * f for v, f in zip(stats, w)])
+            inv = 1.0 / jnp.where(total > 0, total, 1.0)
             w = [v * inv for v in w]
             rest = jnp.zeros((BLOCK_TOKENS - 32, BLOCK_TOKENS), jnp.float32)
             w = jnp.concatenate(w + [rest], 0).T
@@ -220,7 +269,7 @@
             c.wait_send()
 
 
-def send_back(o, lse):
+def send_back(o, stats):
     dma = pltpu.SemaphoreType.DMA
     any_spec = pl.BlockSpec(memory_space=pl.ANY)
     return pl.pallas_call(
@@ -230,13 +279,13 @@
         out_shape=jax.ShapeDtypeStruct((BLOCK_TOKENS, 4 * QCOLS), jnp.bfloat16),
         scratch_shapes=[
             pltpu.VMEM((2, 2, 4, BLOCK_TOKENS, QCOLS), jnp.bfloat16),
-            pltpu.VMEM((2, 2, 4, 8, BLOCK_TOKENS), jnp.float32),
+            pltpu.VMEM((2, 2, 4, 16, BLOCK_TOKENS), jnp.float32),
             dma((16,)), dma((16,)), dma((16,)), dma((16,)),
         ],
         compiler_params=pltpu.CompilerParams(
             collective_id=1, has_side_effects=True, vmem_limit_bytes=16 * 1024 * 1024
         ),
-    )(o, lse)
+    )(o, stats)
 
 
 def copy_to(src, dst, sems, device):
@@ -370,7 +419,7 @@
         ref = meta_all.at[h, ring[a][1 - d] if relay else at[a]]
         i = (h * 2 + d) * 2 + relay
         return copy_to(
-            ref if relay else meta_own, ref, (t_send.at[i], t_recv.at[i]), {a: ring[a][d]}
+            ref if relay else meta_own.at[h], ref, (t_send.at[i], t_recv.at[i]), {a: ring[a][d]}
         )
 
     def start(c):
@@ -406,20 +455,36 @@
     for c in loads[3:]:
         c.wait()
     meta_own[...] = jnp.zeros_like(meta_own)
-    meta_own[0:2, 0:FMAX] = owners_in[...]
-    owners = meta_own[...]
+    meta_own[0, 0:2, 0:FMAX] = owners_in[...]
+    owners = meta_own[0]
     shard = (at["y"] * NZ + at["z"]) * NX + at["x"]
     listed = pairs_in[pl.ds(jnp.minimum(shard, SHARDS - 1 - shard), 1), :]
     half = jnp.take_along_axis(jnp.broadcast_to(listed, (8, 128)), owners, axis=1) & 1
     row = lax.broadcasted_iota(jnp.int32, (8, 128), 0)
     lane = lax.broadcasted_iota(jnp.int32, (8, 128), 1)
     count = jnp.where(row == 0, counts_in[0], jnp.where(row == 1, counts_in[1], 0))
-    meta_own[...] = jnp.where(lane < count, owners * 2 + half, -1)
+    place, rest = lane >> 4, lane & (FMAX - 1)
+    lists = [jnp.zeros((8, 128), jnp.int32)] * 2
+    found = [jnp.zeros((8, 128), jnp.int32)] * 2
+    for j in range(FMAX):
+        owner, which, live = (
+            jnp.sum(jnp.where(lane == j, v, 0), axis=1, keepdims=True)
+            for v in (owners, half, (lane < count).astype(jnp.int32))
+        )
+        oy, oz, ox = owner >> 5, (owner >> 2) & 7, owner & 3
+        for h, (holder, spot) in enumerate(((ox, oy), (oy, ox))):
+            hit = jnp.logical_and(holder == place, live > 0)
+            put = jnp.logical_and(hit, jnp.logical_or(found[h] == 0, found[h] == rest))
+            lists[h] = jnp.where(put, oz * 8 + spot * 2 + which, lists[h])
+            found[h] = found[h] + hit.astype(jnp.int32)
+    for h in range(2):
+        meta_own[h, 0:2] = lists[h][0:2]
+        meta_own[h, 2:4] = found[h][0:2]
     for h, d in both:
         start(t_copy(h, d, 0))
     for h in range(2):
         keep(q_own.at[h], q_all.at[h, at[cross[h]]])
-        keep(meta_own, meta_all.at[h, at[cross[h]]])
+        keep(meta_own.at[h], meta_all.at[h, at[cross[h]]])
 
     def arrived(kind, i, h):
         for d in range(2):
@@ -487,7 +552,7 @@
         + [
             pltpu.VMEM((2, 2 * BLOCK_TOKENS, QCOLS), jnp.bfloat16),
             pltpu.VMEM((2, MAIN + LAST, HEAD_WIDTH), jnp.bfloat16),
-            pltpu.VMEM((8, 128), jnp.int32),
+            pltpu.VMEM((2, 8, 128), jnp.int32),
         ]
         + [dma((n,)) for n in (5, 6, 16, 16, 32, 32, 32, 32, 16, 16, 4, 4, 4, 4, 4, 4, 4, 4, 8, 8)],
         compiler_params=pltpu.CompilerParams(
@@ -497,9 +562,9 @@
 
 
 def on_device(queries, keys, values, far_owners, far_counts, pair_blocks):
-    q, kv, meta = gather_all(queries, keys, values, far_owners, far_counts, pair_blocks)
-    o, lse = attend(meta.reshape(-1), q, kv)
-    return send_back(o, lse)
+    q, kv, codes = gather_all(queries, keys, values, far_owners, far_counts, pair_blocks)
+    o, stats = attend(codes.reshape(-1), q, kv)
+    return send_back(o, stats)
 
 
 def solution(mesh):

time: 100 us -> 96.4 us (0.964)
  Pallas kernels: 98.9 us -> 94.7 us
    pallas_call x1, Pallas kernels: 26.5 us -> 21.2 us  [attend(): pl.pallas_call(attend_kernel, in_specs=[pl.BlockSpec(memory_space=pltpu.S...]
    pallas_call x1, Pallas kernels: 25.4 us -> 26.5 us  [send_back(): pl.pallas_call(return_kernel, in_specs=[any_spec] * 2, out_specs=pl.Block...]
where the time goes in v2:
time: 96.4 us; the launch traced here: 96.3 us
  Pallas kernels  94.7 us (98%)
  local copies, waits for them, and re-layouts  1.49 us (2%)
    pallas_call x1, Pallas kernels, gather_all(): pl.pallas_call(gather_kernel, in_specs=[any_spec] * 5 + [pl.BlockSpec(mem...  47 us
    pallas_call x1, Pallas kernels, send_back(): pl.pallas_call(return_kernel, in_specs=[any_spec] * 2, out_specs=pl.Block...  26.5 us
    pallas_call x1, Pallas kernels, attend(): pl.pallas_call(attend_kernel, in_specs=[pl.BlockSpec(memory_space=pltpu.S...  21.2 us

profile of v2, /device:TPU:65, one launch (start us, length us, event | category | flops | bytes accessed | tf_op | source)
XLA Modules:
  0.0 96.3 jit_solution(12169382441323884086)
XLA Ops:
  0.0 0.0 copy-start
  0.0 0.7 copy-done
  0.7 47.0 %shard_map.64 = (bf16[2,4,256,640]{3,2,1,0:T(8,128)(2,1)S(1)}, bf16[2,32,512,128]{3,2,1,0:T(8,128)(2,1)S(1)}, s32[2,4,8,128]{3,2,1,0:T(8,128)S(1)}) custom-call(bf16[256,1280]{1,0:T(8,128)(2,1)} %q_hbm.1, bf16[256,256]{1,0:T(8,128)(2,1)} %k_hbm.1, bf16[256,256]{1,0:T(8,128)(2,1)} %v_hbm.1, s32[2,16]{1,0:T(2,128)} %owners_hbm.1, s32[64,128]{1,0:T(8,128)} %pairs_hbm.1, ...), custom_call_target="tpu_custom_call" | custom-call | tf_op jit(solution)/shard_map/pallas_call | solution.py:542
  47.7 21.2 %shard_map.65 = (bf16[16,128,640]{2,1,0:T(8,128)(2,1)S(1)}, f32[16,16,128]{2,1,0:T(8,128)S(1)}) custom-call(s32[8192]{0:T(1024)S(1)} %bitcast.1, bf16[2,4,256,640]{3,2,1,0:T(8,128)(2,1)S(1)} %get-tuple-element.11.q_in, bf16[2,32,512,128]{3,2,1,0:T(8,128)(2,1)S(1)} %get-tuple-element.12.kv_in), custom_call_target="tpu_custom_call" | custom-call | tf_op jit(solution)/shard_map/pallas_call | solution.py:181
  68.9 26.5 %shard_map.66 = bf16[128,2560]{1,0:T(8,128)(2,1)S(1)} custom-call(bf16[16,128,640]{2,1,0:T(8,128)(2,1)S(1)} %get-tuple-element.13.o_in, f32[16,16,128]{2,1,0:T(8,128)S(1)} %get-tuple-element.14.stat_in), custom_call_target="tpu_custom_call" | custom-call | tf_op jit(solution)/shard_map/pallas_call | solution.py:275
  95.4 0.8 copy.8
Async XLA Ops:
  0.0 0.7 copy-start

commit v3 on v2

--- a/solution.py
+++ b/solution.py
@@ -198,89 +198,157 @@
     )(codes, q, kv)
 
 
-def return_kernel(o_in, stat_in, out_ref, o_got, stat_got, send, recv, stat_send, stat_recv):
+def columns(rows):
+    rest = jnp.zeros((BLOCK_TOKENS - 8 * len(rows), BLOCK_TOKENS), jnp.float32)
+    return jnp.concatenate([*rows, rest], 0).T
+
+
+def combine(parts, w, g):
+    cols = slice(g * HEAD_WIDTH, (g + 1) * HEAD_WIDTH)
+    return sum(
+        part[:, cols].astype(jnp.float32) * w[:, i * 8 + g : i * 8 + g + 1]
+        for i, part in enumerate(parts)
+    )
+
+
+def return_kernel(
+    o_in, stat_in, out_ref,
+    o_got, stat_got, o_relay, stat_relay, o_mine, stat_mine, o_sum, stat_sum,
+    send, recv, relay_send, relay_recv, own_sem,
+):
     at = {"x": lax.axis_index("x"), "y": lax.axis_index("y")}
     core = lax.axis_index("head")
     axes = ("x", "y")
-    others = [(p, step, e) for step in (1, 3, 2, 0) for e in range(2) for p in range(2)]
-    others = [v for v in others if v[1:] != (0, 0)]
-
-    def device(p, step, e):
-        a = axes[p]
-        return {a: (at[a] + step) % 4, "head": (core + e) % 2}
+
+    def chip(p, step):
+        return (at[axes[p]] + step) % 4
 
     barrier = pltpu.get_barrier_semaphore()
-    met = [v for v in others if v != (1, 0, 1)]
-    for v in met:
-        pl.semaphore_signal(
-            barrier, inc=1, device_id=device(*v), device_id_type=pl.DeviceIdType.MESH
-        )
-    pl.semaphore_wait(barrier, len(met))
-
-    def copies(p, step, e):
-        a = axes[p]
-        target, row = (at[a] + step) % 4, (core + e) % 2
-        i = (p * 4 + step) * 2 + e
-        parts = (
-            (o_in.at[(p * 4 + target) * 2 + row], o_got.at[p, core, at[a]], send, recv),
-            (stat_in.at[(p * 4 + target) * 2 + row], stat_got.at[p, core, at[a]], stat_send, stat_recv),
-        )
-        if step == 0 and e == 0:
-            return [pltpu.make_async_copy(s, d, r.at[i]) for s, d, _, r in parts]
+    met = [{axes[p]: chip(p, step), "head": k} for p in range(2) for step in (1, 3) for k in range(2)]
+    met.append({"head": 1 - core})
+    for device in met:
+        pl.semaphore_signal(barrier, inc=1, device_id=device, device_id_type=pl.DeviceIdType.MESH)
+
+    def item(p, step, row):
+        return (p * 4 + chip(p, step)) * 2 + row
+
+    def own_copies(p, row):
+        i = item(p, 3 if row == 0 else 1, row)
         return [
-            pltpu.make_async_remote_copy(
-                src_ref=s, dst_ref=d, send_sem=w.at[i], recv_sem=r.at[i],
-                device_id=device(p, step, e), device_id_type=pl.DeviceIdType.MESH,
-            )
-            for s, d, w, r in parts
-        ]
-
-    for v in others + [(0, 0, 0), (1, 0, 0)]:
-        for c in copies(*v):
+            pltpu.make_async_copy(o_in.at[i], o_mine.at[p, row], own_sem.at[p, row, 0]),
+            pltpu.make_async_copy(stat_in.at[i], stat_mine.at[p, row], own_sem.at[p, row, 1]),
+        ]
+
+    def kept_copies(p):
+        i = item(p, 0, core)
+        return [
+            pltpu.make_async_copy(o_in.at[i], o_got.at[p, core, 2], own_sem.at[p, 2, 0]),
+            pltpu.make_async_copy(stat_in.at[i], stat_got.at[p, core, 2], own_sem.at[p, 2, 1]),
+        ]
+
+    def relay_copies(p, row):
+        i = item(p, 2, row)
+        device = {axes[p]: chip(p, 3 if row == 0 else 1)}
+        return [
+            copy_to(src.at[i], dst.at[p, row], (relay_send.at[p, row, n], relay_recv.at[p, row, n]), device)
+            for n, (src, dst) in enumerate(((o_in, o_relay), (stat_in, stat_relay)))
+        ]
+
+    def copies(p, place, row, o_src, stat_src, n):
+        device = {"head": row} if place == 2 else {axes[p]: chip(p, 3 - 2 * place), "head": row}
+        return [
+            copy_to(src, dst.at[p, core, place], (send.at[p, n, k], recv.at[p, place, core, k]), device)
+            for k, (src, dst) in enumerate(((o_src, o_got), (stat_src, stat_got)))
+        ]
+
+    def plain(p, place):
+        row = (1, 0, 1 - core)[place]
+        i = item(p, (3, 1, 0)[place], row)
+        return copies(p, place, row, o_in.at[i], stat_in.at[i], place)
+
+    def summed(p, row):
+        return copies(p, row, row, o_sum.at[p, row], stat_sum.at[p, row], 3 + row)
+
+    both = [(p, row) for row in range(2) for p in range(2)]
+    for p, row in both:
+        for c in own_copies(p, row):
             c.start()
     for p in range(2):
-        for e in range(2):
-            for step in range(4):
-                for c in copies(p, step, e):
-                    if (step, e) == (0, 0):
-                        c.wait()
-                    else:
-                        c.wait_recv()
+        for c in kept_copies(p):
+            c.start()
+    pl.semaphore_wait(barrier, len(met))
+    for p, row in both:
+        for c in relay_copies(p, row):
+            c.start()
+    for place in range(3):
+        for p in range(2):
+            for c in plain(p, place):
+                c.start()
+    for p, row in both:
+        for c in own_copies(p, row):
+            c.wait()
+        for c in relay_copies(p, row):
+            c.wait_recv()
+        stats = [stat_mine[p, row], stat_relay[p, row]]
+        top = jnp.maximum(stats[0][:8], stats[1][:8])
+        f = [jnp.exp2(v[:8] - top) for v in stats]
+        stat_sum[p, row, 0:8] = top
+        stat_sum[p, row, 8:16] = stats[0][8:] * f[0] + stats[1][8:] * f[1]
+        w = columns(f)
+        for g in range(GROUP):
+            cols = slice(g * HEAD_WIDTH, (g + 1) * HEAD_WIDTH)
+            mixed = combine([o_mine.at[p, row], o_relay.at[p, row]], w, g)
+            o_sum[p, row, :, cols] = mixed.astype(jnp.bfloat16)
+        for c in summed(p, row):
+            c.start()
+
+    def arrival(p, place, c, k):
+        dst = (o_got, stat_got)[k].at[p, c, place]
+        return copy_to(dst, dst, (send.at[p, 0, k], recv.at[p, place, c, k]), {"head": 1 - core})
+
     for p in range(2):
+        for c in kept_copies(p):
+            c.wait()
+        for k in range(2):
+            arrival(p, 2, 1 - core, k).wait_recv()
+            for c in range(2):
+                for place in range(2):
+                    arrival(p, place, c, k).wait_recv()
         for c in range(2):
-            stats = [stat_got[p, c, i] for i in range(4)]
+            stats = [stat_got[p, c, i] for i in range(3)]
             top = functools.reduce(jnp.maximum, [v[:8] for v in stats])
-            w = [jnp.exp2(v[:8] - top) for v in stats]
-            total = functools.reduce(jnp.add, [v[8:] * f for v, f in zip(stats, w)])
+            f = [jnp.exp2(v[:8] - top) for v in stats]
+            total = functools.reduce(jnp.add, [v[8:] * u for v, u in zip(stats, f)])
             inv = 1.0 / jnp.where(total > 0, total, 1.0)
-            w = [v * inv for v in w]
-            rest = jnp.zeros((BLOCK_TOKENS - 32, BLOCK_TOKENS), jnp.float32)
-            w = jnp.concatenate(w + [rest], 0).T
+            w = columns([v * inv for v in f])
             for g in range(GROUP):
-                cols = slice(g * HEAD_WIDTH, (g + 1) * HEAD_WIDTH)
-                mixed = sum(
-                    o_got[p, c, i, :, cols].astype(jnp.float32) * w[:, i * 8 + g : i * 8 + g + 1]
-                    for i in range(4)
-                )
                 start = (c * 2 + p) * QCOLS + g * HEAD_WIDTH
+                mixed = combine([o_got.at[p, c, i] for i in range(3)], w, g)
                 out_ref[:, start : start + HEAD_WIDTH] = mixed.astype(jnp.bfloat16)
-    for v in others:
-        for c in copies(*v):
+    for p, row in both:
+        for c in relay_copies(p, row) + summed(p, row):
             c.wait_send()
+    for p in range(2):
+        for place in range(3):
+            for c in plain(p, place):
+                c.wait_send()
 
 
 def send_back(o, stats):
     dma = pltpu.SemaphoreType.DMA
     any_spec = pl.BlockSpec(memory_space=pl.ANY)
+    partial, figures = (BLOCK_TOKENS, QCOLS), (16, BLOCK_TOKENS)
+    pairs = [pltpu.VMEM((2, 2, *partial), jnp.bfloat16), pltpu.VMEM((2, 2, *figures), jnp.float32)]
     return pl.pallas_call(
         return_kernel,
         in_specs=[any_spec] * 2,
         out_specs=pl.BlockSpec(memory_space=pltpu.VMEM),
         out_shape=jax.ShapeDtypeStruct((BLOCK_TOKENS, 4 * QCOLS), jnp.bfloat16),
         scratch_shapes=[
-            pltpu.VMEM((2, 2, 4, BLOCK_TOKENS, QCOLS), jnp.bfloat16),
-            pltpu.VMEM((2, 2, 4, 16, BLOCK_TOKENS), jnp.float32),
-            dma((16,)), dma((16,)), dma((16,)), dma((16,)),
+            pltpu.VMEM((2, 2, 3, *partial), jnp.bfloat16),
+            pltpu.VMEM((2, 2, 3, *figures), jnp.float32),
+            *(pairs * 3),
+            dma((2, 5, 2)), dma((2, 3, 2, 2)), dma((2, 2, 2)), dma((2, 2, 2)), dma((2, 3, 2)),
         ],
         compiler_params=pltpu.CompilerParams(
             collective_id=1, has_side_effects=True, vmem_limit_bytes=16 * 1024 * 1024

time: 96.4 us -> 93.3 us (0.968)
  Pallas kernels: 94.7 us -> 91.7 us
    pallas_call x1, Pallas kernels: 26.5 us -> 21.7 us  [send_back(): pl.pallas_call(return_kernel, in_specs=[any_spec] * 2, out_specs=pl.Block...]
    pallas_call x1, Pallas kernels: 21.2 us -> 22.9 us  [attend(): pl.pallas_call(attend_kernel, in_specs=[pl.BlockSpec(memory_space=pltpu.S...]
where the time goes in v3:
time: 93.3 us; the launch traced here: 93.2 us
  Pallas kernels  91.7 us (98%)
  local copies, waits for them, and re-layouts  1.49 us (2%)
    pallas_call x1, Pallas kernels, gather_all(): pl.pallas_call(gather_kernel, in_specs=[any_spec] * 5 + [pl.BlockSpec(mem...  47 us
    pallas_call x1, Pallas kernels, attend(): pl.pallas_call(attend_kernel, in_specs=[pl.BlockSpec(memory_space=pltpu.S...  22.9 us
    pallas_call x1, Pallas kernels, send_back(): pl.pallas_call(return_kernel, in_specs=[any_spec] * 2, out_specs=pl.Block...  21.7 us

profile of v3, /device:TPU:65, one launch (start us, length us, event | category | flops | bytes accessed | tf_op | source)
XLA Modules:
  0.0 93.2 jit_solution(1333449982896820843)
XLA Ops:
  0.0 0.0 copy-start
  0.0 0.7 copy-done
  0.7 47.0 %shard_map.64 = (bf16[2,4,256,640]{3,2,1,0:T(8,128)(2,1)S(1)}, bf16[2,32,512,128]{3,2,1,0:T(8,128)(2,1)S(1)}, s32[2,4,8,128]{3,2,1,0:T(8,128)S(1)}) custom-call(bf16[256,1280]{1,0:T(8,128)(2,1)} %q_hbm.1, bf16[256,256]{1,0:T(8,128)(2,1)} %k_hbm.1, bf16[256,256]{1,0:T(8,128)(2,1)} %v_hbm.1, s32[2,16]{1,0:T(2,128)} %owners_hbm.1, s32[64,128]{1,0:T(8,128)} %pairs_hbm.1, ...), custom_call_target="tpu_custom_call" | custom-call | tf_op jit(solution)/shard_map/pallas_call | solution.py:610
  47.7 22.9 %shard_map.65 = (bf16[16,128,640]{2,1,0:T(8,128)(2,1)S(1)}, f32[16,16,128]{2,1,0:T(8,128)S(1)}) custom-call(s32[8192]{0:T(1024)S(1)} %bitcast.1, bf16[2,4,256,640]{3,2,1,0:T(8,128)(2,1)S(1)} %get-tuple-element.11.q_in, bf16[2,32,512,128]{3,2,1,0:T(8,128)(2,1)S(1)} %get-tuple-element.12.kv_in), custom_call_target="tpu_custom_call" | custom-call | tf_op jit(solution)/shard_map/pallas_call | solution.py:181
  70.6 21.7 %shard_map.66 = bf16[128,2560]{1,0:T(8,128)(2,1)S(1)} custom-call(bf16[16,128,640]{2,1,0:T(8,128)(2,1)S(1)} %get-tuple-element.13.o_in, f32[16,16,128]{2,1,0:T(8,128)S(1)} %get-tuple-element.14.stat_in), custom_call_target="tpu_custom_call" | custom-call | tf_op jit(solution)/shard_map/pallas_call | solution.py:342
  92.3 0.8 copy.8
Async XLA Ops:
  0.0 0.7 copy-start

commit v4 on v3

--- a/solution.py
+++ b/solution.py
@@ -34,7 +34,7 @@
             for i, (src, dst) in enumerate(((q_in, q_ref), (kv_in, kv_ref)))
         ]
 
-    for c in loads(0) + loads(1):
+    for c in loads(0):
         c.start()
 
     def base_of(pattern, item):
@@ -124,6 +124,9 @@
     for pattern, begin, stop in ((0, 0, middle), (1, middle, end)):
         for c in loads(pattern):
             c.wait()
+        if pattern == 0:
+            for c in loads(1):
+                c.start()
         for row in range(2):
             own_blocks(pattern, row)
 
@@ -378,8 +381,8 @@
 
 
 def gather_kernel(
-    q_hbm, k_hbm, v_hbm, owners_hbm, pairs_hbm, counts_in, q_all, kv_all, meta_all,
-    q_in, k_in, v_in, owners_in, pairs_in, q_own, kv_own, meta_own, in_sem, local_sem,
+    q_hbm, k_hbm, v_hbm, owners_hbm, pairs_hbm, counts_hbm, q_all, kv_all, meta_all,
+    q_in, k_in, v_in, owners_in, pairs_in, counts_in, q_own, kv_own, meta_own, in_sem, local_sem,
     z_send, z_recv, near_send, near_recv, far_send, far_recv,
     lz_send, lz_recv, ln_send, ln_recv, lf_send, lf_recv,
     q_send, q_recv, qf_send, qf_recv, t_send, t_recv,
@@ -400,7 +403,7 @@
         for i, (src, dst) in enumerate(
             (
                 (k_hbm, k_in), (v_hbm, v_in), (q_hbm, q_in),
-                (owners_hbm, owners_in), (pairs_hbm, pairs_in),
+                (owners_hbm, owners_in), (pairs_hbm, pairs_in), (counts_hbm, counts_in),
             )
         )
     ]
@@ -606,10 +609,10 @@
 def gather_all(q, k, v, owners, counts, pairs):
     dma = pltpu.SemaphoreType.DMA
     any_spec = pl.BlockSpec(memory_space=pl.ANY)
-    arrays = [pltpu.with_memory_space_constraint(a, pltpu.HBM) for a in (q, k, v, owners, pairs)]
+    arrays = [pltpu.with_memory_space_constraint(a, pltpu.HBM) for a in (q, k, v, owners, pairs, counts)]
     return pl.pallas_call(
         gather_kernel,
-        in_specs=[any_spec] * 5 + [pl.BlockSpec(memory_space=pltpu.SMEM)],
+        in_specs=[any_spec] * 6,
         out_specs=[any_spec] * 3,
         out_shape=[
             jax.ShapeDtypeStruct((2, 4, 2 * BLOCK_TOKENS, QCOLS), jnp.bfloat16),
@@ -618,15 +621,16 @@
         ],
         scratch_shapes=[pltpu.VMEM(a.shape, a.dtype) for a in (q, k, v, owners, pairs)]
         + [
+            pltpu.SMEM(counts.shape, counts.dtype),
             pltpu.VMEM((2, 2 * BLOCK_TOKENS, QCOLS), jnp.bfloat16),
             pltpu.VMEM((2, MAIN + LAST, HEAD_WIDTH), jnp.bfloat16),
             pltpu.VMEM((2, 8, 128), jnp.int32),
         ]
-        + [dma((n,)) for n in (5, 6, 16, 16, 32, 32, 32, 32, 16, 16, 4, 4, 4, 4, 4, 4, 4, 4, 8, 8)],
+        + [dma((n,)) for n in (6, 6, 16, 16, 32, 32, 32, 32, 16, 16, 4, 4, 4, 4, 4, 4, 4, 4, 8, 8)],
         compiler_params=pltpu.CompilerParams(
             collective_id=0, has_side_effects=True, vmem_limit_bytes=16 * 1024 * 1024
         ),
-    )(*arrays, counts)
+    )(*arrays)
 
 
 def on_device(queries, keys, values, far_owners, far_counts, pair_blocks):

time: 93.3 us -> 90.9 us (0.974)
  Pallas kernels: 91.7 us -> 89.9 us
    pallas_call x1, Pallas kernels: 22.9 us -> 21.8 us  [attend(): pl.pallas_call(attend_kernel, in_specs=[pl.BlockSpec(memory_space=pltpu.S...]
where the time goes in v4:
time: 90.9 us; the launch traced here: 90.8 us
  Pallas kernels  89.9 us (99%)
    pallas_call x1, Pallas kernels, gather_all(): pl.pallas_call(gather_kernel, in_specs=[any_spec] * 6, out_specs=[any_spe...  46.4 us
    pallas_call x1, Pallas kernels, attend(): pl.pallas_call(attend_kernel, in_specs=[pl.BlockSpec(memory_space=pltpu.S...  21.8 us
    pallas_call x1, Pallas kernels, send_back(): pl.pallas_call(return_kernel, in_specs=[any_spec] * 2, out_specs=pl.Block...  21.7 us

profile of v4, /device:TPU:65, one launch (start us, length us, event | category | flops | bytes accessed | tf_op | source)
XLA Modules:
  0.0 90.8 jit_solution(1482052078637972579)
XLA Ops:
  0.0 46.4 %shard_map.64 = (bf16[2,4,256,640]{3,2,1,0:T(8,128)(2,1)S(1)}, bf16[2,32,512,128]{3,2,1,0:T(8,128)(2,1)S(1)}, s32[2,4,8,128]{3,2,1,0:T(8,128)S(1)}) custom-call(bf16[256,1280]{1,0:T(8,128)(2,1)} %q_hbm.1, bf16[256,256]{1,0:T(8,128)(2,1)} %k_hbm.1, bf16[256,256]{1,0:T(8,128)(2,1)} %v_hbm.1, s32[2,16]{1,0:T(2,128)} %owners_hbm.1, s32[64,128]{1,0:T(8,128)} %pairs_hbm.1, ...), custom_call_target="tpu_custom_call" | custom-call | tf_op jit(solution)/shard_map/pallas_call | solution.py:613
  46.4 21.8 %shard_map.65 = (bf16[16,128,640]{2,1,0:T(8,128)(2,1)S(1)}, f32[16,16,128]{2,1,0:T(8,128)S(1)}) custom-call(s32[8192]{0:T(1024)S(1)} %bitcast.1, bf16[2,4,256,640]{3,2,1,0:T(8,128)(2,1)S(1)} %get-tuple-element.11.q_in, bf16[2,32,512,128]{3,2,1,0:T(8,128)(2,1)S(1)} %get-tuple-element.12.kv_in), custom_call_target="tpu_custom_call" | custom-call | tf_op jit(solution)/shard_map/pallas_call | solution.py:184
  68.2 21.7 %shard_map.66 = bf16[128,2560]{1,0:T(8,128)(2,1)S(1)} custom-call(bf16[16,128,640]{2,1,0:T(8,128)(2,1)S(1)} %get-tuple-element.13.o_in, f32[16,16,128]{2,1,0:T(8,128)S(1)} %get-tuple-element.14.stat_in), custom_call_target="tpu_custom_call" | custom-call | tf_op jit(solution)/shard_map/pallas_call | solution.py:345
  89.9 0.8 copy.8

commit v5 on v4

--- a/solution.py
+++ b/solution.py
@@ -53,6 +53,14 @@
     middle = lax.fori_loop(0, 8, functools.partial(build, 0), jnp.int32(0))
     end = lax.fori_loop(8, 16, functools.partial(build, 1), middle)
 
+    def clear(item, carry):
+        m_ref[item] = jnp.full((QCOLS, HEAD_WIDTH), NEG, jnp.float32)
+        l_ref[item] = jnp.zeros((QCOLS, HEAD_WIDTH), jnp.float32)
+        acc_ref[item] = jnp.zeros((QCOLS, HEAD_WIDTH), jnp.float32)
+        return carry
+
+    lax.fori_loop(0, ITEMS, clear, 0)
+
     def score(pattern, item, blocks):
         tokens = pl.ds(pl.multiple_of((item & 1) * BLOCK_TOKENS, BLOCK_TOKENS), BLOCK_TOKENS)
         q = q_ref.at[pattern, (item >> 1) & 3, tokens]
@@ -103,13 +111,11 @@
         item, i = code >> 4, code & 15
         at = base_of(pattern, item) + i * STEP
         blocks = [codes_ref[at + k] for k in range(STEP)]
-        own = ((item >> 1) & 3) == (x if pattern == 0 else y)
-        fresh = jnp.logical_and(i == 0, jnp.logical_not(own))
-        return item, blocks, count_ref[item] - i * STEP, fresh
-
-    def absorb(pattern, s, item, blocks, left, fresh):
+        return item, blocks, count_ref[item] - i * STEP
+
+    def absorb(pattern, s, item, blocks, left):
         parts = split(s)
-        m_old = jnp.where(fresh, NEG, m_ref[item])
+        m_old = m_ref[item]
         m_new = jnp.maximum(m_old, top_of(parts))
         alpha = jnp.exp2((m_old - m_new) * EXP_SCALE)
         off = m_new * EXP_SCALE
@@ -118,8 +124,8 @@
             for i, v in enumerate(parts)
         ]
         m_ref[item] = m_new
-        l_ref[item] = jnp.where(fresh, 0.0, l_ref[item]) * alpha + functools.reduce(jnp.add, p)
-        acc_ref[item] = jnp.where(fresh, 0.0, acc_ref[item]) * alpha + mix(pattern, blocks, p)
+        l_ref[item] = l_ref[item] * alpha + functools.reduce(jnp.add, p)
+        acc_ref[item] = acc_ref[item] * alpha + mix(pattern, blocks, p)
 
     for pattern, begin, stop in ((0, 0, middle), (1, middle, end)):
         for c in loads(pattern):
@@ -149,32 +155,18 @@
     lane = lax.broadcasted_iota(jnp.int32, (BLOCK_TOKENS, BLOCK_TOKENS), 1)
 
     def close(item, carry):
-        own = ((item >> 1) & 3) == jnp.where(item < 8, x, y)
-        read = jnp.logical_or(own, count_ref[item] > 0)
-
-        @pl.when(read)
-        def _():
-            tops = jnp.zeros((BLOCK_TOKENS, BLOCK_TOKENS), jnp.float32)
-            sums = jnp.zeros((BLOCK_TOKENS, BLOCK_TOKENS), jnp.float32)
-            for g in range(GROUP):
-                part = slice(g * HEAD_WIDTH, (g + 1) * HEAD_WIDTH)
-                o_ref[item, :, part] = acc_ref[item, part].astype(jnp.bfloat16)
-                tops = jnp.where(lane == g, m_ref[item, part], tops)
-                sums = jnp.where(
-                    lane == g, jnp.sum(l_ref[item, part], axis=1, keepdims=True), sums
-                )
-            stat_ref[item, 0:8] = tops.T[:8] * EXP_SCALE
-            stat_ref[item, 8:16] = sums.T[:8]
-
-        @pl.when(jnp.logical_not(read))
-        def _():
-            o_ref[item] = jnp.zeros((BLOCK_TOKENS, QCOLS), jnp.bfloat16)
-            stat_ref[item, 0:8] = jnp.full((8, BLOCK_TOKENS), NEG, jnp.float32)
-            stat_ref[item, 8:16] = jnp.zeros((8, BLOCK_TOKENS), jnp.float32)
-
+        tops = jnp.zeros((BLOCK_TOKENS, BLOCK_TOKENS), jnp.float32)
+        sums = jnp.zeros((BLOCK_TOKENS, BLOCK_TOKENS), jnp.float32)
+        for g in range(GROUP):
+            part = slice(g * HEAD_WIDTH, (g + 1) * HEAD_WIDTH)
+            o_ref[item, :, part] = acc_ref[item, part].astype(jnp.bfloat16)
+            tops = jnp.where(lane == g, m_ref[item, part], tops)
+            sums = jnp.where(lane == g, jnp.sum(l_ref[item, part], axis=1, keepdims=True), sums)
+        stat_ref[item, 0:8] = tops.T[:8] * EXP_SCALE
+        stat_ref[item, 8:16] = sums.T[:8]
         return carry
 
-    lax.fori_loop(0, ITEMS, close, 0)
+    lax.fori_loop(0, ITEMS, close, 0, unroll=2)
 
 
 def attend(codes, q, kv):

time: 90.9 us -> 92.2 us (1.014)
  Pallas kernels: 89.9 us -> 91.3 us
    pallas_call x1, Pallas kernels: 21.8 us -> 23.1 us  [attend(): pl.pallas_call(attend_kernel, in_specs=[pl.BlockSpec(memory_space=pltpu.S...]
where the time goes in v5:
time: 92.2 us; the launch traced here: 92.1 us
  Pallas kernels  91.3 us (99%)
    pallas_call x1, Pallas kernels, gather_all(): pl.pallas_call(gather_kernel, in_specs=[any_spec] * 6, out_specs=[any_spe...  46.4 us
    pallas_call x1, Pallas kernels, attend(): pl.pallas_call(attend_kernel, in_specs=[pl.BlockSpec(memory_space=pltpu.S...  23.1 us
    pallas_call x1, Pallas kernels, send_back(): pl.pallas_call(return_kernel, in_specs=[any_spec] * 2, out_specs=pl.Block...  21.7 us

profile of v5, /device:TPU:65, one launch (start us, length us, event | category | flops | bytes accessed | tf_op | source)
XLA Modules:
  0.0 92.1 jit_solution(4987631043594501721)
XLA Ops:
  0.0 46.4 %shard_map.64 = (bf16[2,4,256,640]{3,2,1,0:T(8,128)(2,1)S(1)}, bf16[2,32,512,128]{3,2,1,0:T(8,128)(2,1)S(1)}, s32[2,4,8,128]{3,2,1,0:T(8,128)S(1)}) custom-call(bf16[256,1280]{1,0:T(8,128)(2,1)} %q_hbm.1, bf16[256,256]{1,0:T(8,128)(2,1)} %k_hbm.1, bf16[256,256]{1,0:T(8,128)(2,1)} %v_hbm.1, s32[2,16]{1,0:T(2,128)} %owners_hbm.1, s32[64,128]{1,0:T(8,128)} %pairs_hbm.1, ...), custom_call_target="tpu_custom_call" | custom-call | tf_op jit(solution)/shard_map/pallas_call | solution.py:605
  46.4 23.1 %shard_map.65 = (bf16[16,128,640]{2,1,0:T(8,128)(2,1)S(1)}, f32[16,16,128]{2,1,0:T(8,128)S(1)}) custom-call(s32[8192]{0:T(1024)S(1)} %bitcast.1, bf16[2,4,256,640]{3,2,1,0:T(8,128)(2,1)S(1)} %get-tuple-element.11.q_in, bf16[2,32,512,128]{3,2,1,0:T(8,128)(2,1)S(1)} %get-tuple-element.12.kv_in), custom_call_target="tpu_custom_call" | custom-call | tf_op jit(solution)/shard_map/pallas_call | solution.py:176
  69.5 21.7 %shard_map.66 = bf16[128,2560]{1,0:T(8,128)(2,1)S(1)} custom-call(bf16[16,128,640]{2,1,0:T(8,128)(2,1)S(1)} %get-tuple-element.13.o_in, f32[16,16,128]{2,1,0:T(8,128)S(1)} %get-tuple-element.14.stat_in), custom_call_target="tpu_custom_call" | custom-call | tf_op jit(solution)/shard_map/pallas_call | solution.py:337
  91.3 0.8 copy.8

commit v6 on v5

--- a/solution.py
+++ b/solution.py
@@ -54,9 +54,12 @@
     end = lax.fori_loop(8, 16, functools.partial(build, 1), middle)
 
     def clear(item, carry):
-        m_ref[item] = jnp.full((QCOLS, HEAD_WIDTH), NEG, jnp.float32)
-        l_ref[item] = jnp.zeros((QCOLS, HEAD_WIDTH), jnp.float32)
-        acc_ref[item] = jnp.zeros((QCOLS, HEAD_WIDTH), jnp.float32)
+        @pl.when(((item >> 1) & 3) != jnp.where(item < 8, x, y))
+        def _():
+            m_ref[item] = jnp.full((QCOLS, HEAD_WIDTH), NEG, jnp.float32)
+            l_ref[item] = jnp.zeros((QCOLS, HEAD_WIDTH), jnp.float32)
+            acc_ref[item] = jnp.zeros((QCOLS, HEAD_WIDTH), jnp.float32)
+
         return carry
 
     lax.fori_loop(0, ITEMS, clear, 0)
@@ -136,21 +139,18 @@
         for row in range(2):
             own_blocks(pattern, row)
 
-        def several(j, carry, pattern=pattern, begin=begin):
-            got = [fetch(pattern, begin + j * UNROLL + u) for u in range(UNROLL)]
-            scores = [score(pattern, g[0], g[1]) for g in got]
-            for g, s in zip(got, scores):
-                absorb(pattern, s, *g)
-            return carry
-
-        def single(c, carry, pattern=pattern):
-            g = fetch(pattern, c)
-            absorb(pattern, score(pattern, g[0], g[1]), *g)
-            return carry
-
-        whole = (stop - begin) // UNROLL
-        lax.fori_loop(0, whole, several, 0)
-        lax.fori_loop(begin + whole * UNROLL, stop, single, 0)
+        for width in (UNROLL, 2, 1):
+
+            def several(j, carry, pattern=pattern, begin=begin, width=width):
+                got = [fetch(pattern, begin + j * width + u) for u in range(width)]
+                scores = [score(pattern, g[0], g[1]) for g in got]
+                for g, s in zip(got, scores):
+                    absorb(pattern, s, *g)
+                return carry
+
+            turns = (stop - begin) // width
+            lax.fori_loop(0, turns, several, 0)
+            begin = begin + turns * width
 
     lane = lax.broadcasted_iota(jnp.int32, (BLOCK_TOKENS, BLOCK_TOKENS), 1)
 
@@ -208,7 +208,7 @@
 
 def return_kernel(
     o_in, stat_in, out_ref,
-    o_got, stat_got, o_relay, stat_relay, o_mine, stat_mine, o_sum, stat_sum,
+    o_got, stat_got, o_early, o_relay, stat_relay, o_mine, stat_mine, o_sum, stat_sum,
     send, recv, relay_send, relay_recv, own_sem,
 ):
     at = {"x": lax.axis_index("x"), "y": lax.axis_index("y")}
@@ -301,24 +301,38 @@
         dst = (o_got, stat_got)[k].at[p, c, place]
         return copy_to(dst, dst, (send.at[p, 0, k], recv.at[p, place, c, k]), {"head": 1 - core})
 
+    tops, sums = {}, {}
     for p in range(2):
         for c in kept_copies(p):
             c.wait()
         for k in range(2):
             arrival(p, 2, 1 - core, k).wait_recv()
             for c in range(2):
-                for place in range(2):
-                    arrival(p, place, c, k).wait_recv()
+                arrival(p, 1 - core, c, k).wait_recv()
         for c in range(2):
-            stats = [stat_got[p, c, i] for i in range(3)]
-            top = functools.reduce(jnp.maximum, [v[:8] for v in stats])
-            f = [jnp.exp2(v[:8] - top) for v in stats]
-            total = functools.reduce(jnp.add, [v[8:] * u for v, u in zip(stats, f)])
+            stats = [stat_got[p, c, 2], stat_got[p, c, 1 - core]]
+            tops[p, c] = jnp.maximum(stats[0][:8], stats[1][:8])
+            f = [jnp.exp2(v[:8] - tops[p, c]) for v in stats]
+            sums[p, c] = stats[0][8:] * f[0] + stats[1][8:] * f[1]
+            w = columns(f)
+            for g in range(GROUP):
+                cols = slice(g * HEAD_WIDTH, (g + 1) * HEAD_WIDTH)
+                o_early[p, c, :, cols] = combine(
+                    [o_got.at[p, c, 2], o_got.at[p, c, 1 - core]], w, g
+                )
+    for p in range(2):
+        for c in range(2):
+            for k in range(2):
+                arrival(p, core, c, k).wait_recv()
+            stat = stat_got[p, c, core]
+            top = jnp.maximum(tops[p, c], stat[:8])
+            f = [jnp.exp2(tops[p, c] - top), jnp.exp2(stat[:8] - top)]
+            total = sums[p, c] * f[0] + stat[8:] * f[1]
             inv = 1.0 / jnp.where(total > 0, total, 1.0)
             w = columns([v * inv for v in f])
             for g in range(GROUP):
                 start = (c * 2 + p) * QCOLS + g * HEAD_WIDTH
-                mixed = combine([o_got.at[p, c, i] for i in range(3)], w, g)
+                mixed = combine([o_early.at[p, c], o_got.at[p, c, core]], w, g)
                 out_ref[:, start : start + HEAD_WIDTH] = mixed.astype(jnp.bfloat16)
     for p, row in both:
         for c in relay_copies(p, row) + summed(p, row):
@@ -342,6 +356,7 @@
         scratch_shapes=[
             pltpu.VMEM((2, 2, 3, *partial), jnp.bfloat16),
             pltpu.VMEM((2, 2, 3, *figures), jnp.float32),
+            pltpu.VMEM((2, 2, *partial), jnp.float32),
             *(pairs * 3),
             dma((2, 5, 2)), dma((2, 3, 2, 2)), dma((2, 2, 2)), dma((2, 2, 2)), dma((2, 3, 2)),
         ],

time: 92.2 us -> 90.6 us (0.983)
  Pallas kernels: 91.3 us -> 89.6 us
    pallas_call x1, Pallas kernels: 23.1 us -> 21.6 us  [attend(): pl.pallas_call(attend_kernel, in_specs=[pl.BlockSpec(memory_space=pltpu.S...]
where the time goes in v6:
time: 90.6 us; the launch traced here: 90.5 us
  Pallas kernels  89.6 us (99%)
    pallas_call x1, Pallas kernels, gather_all(): pl.pallas_call(gather_kernel, in_specs=[any_spec] * 6, out_specs=[any_spe...  46.4 us
    pallas_call x1, Pallas kernels, send_back(): pl.pallas_call(return_kernel, in_specs=[any_spec] * 2, out_specs=pl.Block...  21.6 us
    pallas_call x1, Pallas kernels, attend(): pl.pallas_call(attend_kernel, in_specs=[pl.BlockSpec(memory_space=pltpu.S...  21.6 us

profile of v6, /device:TPU:65, one launch (start us, length us, event | category | flops | bytes accessed | tf_op | source)
XLA Modules:
  0.0 90.5 jit_solution(14697914087117356176)
XLA Ops:
  0.0 46.4 %shard_map.64 = (bf16[2,4,256,640]{3,2,1,0:T(8,128)(2,1)S(1)}, bf16[2,32,512,128]{3,2,1,0:T(8,128)(2,1)S(1)}, s32[2,4,8,128]{3,2,1,0:T(8,128)S(1)}) custom-call(bf16[256,1280]{1,0:T(8,128)(2,1)} %q_hbm.1, bf16[256,256]{1,0:T(8,128)(2,1)} %k_hbm.1, bf16[256,256]{1,0:T(8,128)(2,1)} %v_hbm.1, s32[2,16]{1,0:T(2,128)} %owners_hbm.1, s32[64,128]{1,0:T(8,128)} %pairs_hbm.1, ...), custom_call_target="tpu_custom_call" | custom-call | tf_op jit(solution)/shard_map/pallas_call | solution.py:620
  46.4 21.6 %shard_map.65 = (bf16[16,128,640]{2,1,0:T(8,128)(2,1)S(1)}, f32[16,16,128]{2,1,0:T(8,128)S(1)}) custom-call(s32[8192]{0:T(1024)S(1)} %bitcast.1, bf16[2,4,256,640]{3,2,1,0:T(8,128)(2,1)S(1)} %get-tuple-element.11.q_in, bf16[2,32,512,128]{3,2,1,0:T(8,128)(2,1)S(1)} %get-tuple-element.12.kv_in), custom_call_target="tpu_custom_call" | custom-call | tf_op jit(solution)/shard_map/pallas_call | solution.py:176
  68.0 21.6 %shard_map.66 = bf16[128,2560]{1,0:T(8,128)(2,1)S(1)} custom-call(bf16[16,128,640]{2,1,0:T(8,128)(2,1)S(1)} %get-tuple-element.13.o_in, f32[16,16,128]{2,1,0:T(8,128)S(1)} %get-tuple-element.14.stat_in), custom_call_target="tpu_custom_call" | custom-call | tf_op jit(solution)/shard_map/pallas_call | solution.py:351
  89.7 0.8 copy.8

commit v7 on v6

--- a/solution.py
+++ b/solution.py
@@ -16,7 +16,6 @@
 FMAX = 16
 SLOTS = 32
 ITEMS = 16
-STEP = 2
 UNROLL = 4
 NEG = -1e30
 EXP_SCALE = 1.4426950408889634 * HEAD_WIDTH ** (-0.5)
@@ -24,7 +23,7 @@
 
 def attend_kernel(
     codes_ref, q_in, kv_in, o_ref, stat_ref,
-    count_ref, chunk_ref, q_ref, kv_ref, acc_ref, m_ref, l_ref, sem,
+    count_ref, chunk_ref, single_ref, q_ref, kv_ref, acc_ref, m_ref, l_ref, sem,
 ):
     y, z, x = (lax.axis_index(a) for a in ("y", "z", "x"))
 
@@ -40,7 +39,7 @@
     def base_of(pattern, item):
         return (item >> 1) * 1024 + (item & 1) * 128 + (x if pattern == 0 else y) * FMAX
 
-    def build(pattern, item, chunks):
+    def build(pattern, item, ends):
         n = codes_ref[base_of(pattern, item) + 2 * 128]
         count_ref[item] = n
 
@@ -48,9 +47,11 @@
             chunk_ref[chunks] = item * 16 + i
             return chunks + 1
 
-        return lax.fori_loop(0, (n + STEP - 1) // STEP, note, chunks)
-
-    middle = lax.fori_loop(0, 8, functools.partial(build, 0), jnp.int32(0))
+        single_ref[ends[1]] = item
+        return lax.fori_loop(0, n >> 1, note, ends[0]), ends[1] + (n & 1)
+
+    none = (jnp.int32(0), jnp.int32(0))
+    middle = lax.fori_loop(0, 8, functools.partial(build, 0), none)
     end = lax.fori_loop(8, 16, functools.partial(build, 1), middle)
 
     def clear(item, carry):
@@ -103,34 +104,33 @@
         query_pos = lax.broadcasted_iota(jnp.int32, parts[0].shape, 0) & (BLOCK_TOKENS - 1)
         key_pos = lax.broadcasted_iota(jnp.int32, parts[0].shape, 1)
         parts[-1] = jnp.where(key_pos <= query_pos, parts[-1], NEG)
-        m = top_of(parts)
-        p = [jnp.exp2((v - m) * EXP_SCALE) for v in parts]
+        m = top_of(parts) * EXP_SCALE
+        p = [jnp.exp2(v * EXP_SCALE - m) for v in parts]
         m_ref[item] = jnp.broadcast_to(m, (QCOLS, HEAD_WIDTH))
         l_ref[item] = functools.reduce(jnp.add, p)
         acc_ref[item] = mix(pattern, blocks, p)
 
-    def fetch(pattern, c):
+    def fetch_pair(pattern, c):
         code = chunk_ref[c]
         item, i = code >> 4, code & 15
-        at = base_of(pattern, item) + i * STEP
-        blocks = [codes_ref[at + k] for k in range(STEP)]
-        return item, blocks, count_ref[item] - i * STEP
-
-    def absorb(pattern, s, item, blocks, left):
+        at = base_of(pattern, item) + i * 2
+        return item, [codes_ref[at], codes_ref[at + 1]]
+
+    def fetch_single(pattern, c):
+        item = single_ref[c]
+        return item, [codes_ref[base_of(pattern, item) + count_ref[item] - 1]]
+
+    def absorb(pattern, s, item, blocks):
         parts = split(s)
         m_old = m_ref[item]
-        m_new = jnp.maximum(m_old, top_of(parts))
-        alpha = jnp.exp2((m_old - m_new) * EXP_SCALE)
-        off = m_new * EXP_SCALE
-        p = [
-            jnp.exp2(v * EXP_SCALE - (off if i == 0 else off + jnp.where(left > i, 0.0, -NEG)))
-            for i, v in enumerate(parts)
-        ]
+        m_new = jnp.maximum(m_old, top_of(parts) * EXP_SCALE)
+        alpha = jnp.exp2(m_old - m_new)
+        p = [jnp.exp2(v * EXP_SCALE - m_new) for v in parts]
         m_ref[item] = m_new
         l_ref[item] = l_ref[item] * alpha + functools.reduce(jnp.add, p)
         acc_ref[item] = acc_ref[item] * alpha + mix(pattern, blocks, p)
 
-    for pattern, begin, stop in ((0, 0, middle), (1, middle, end)):
+    for pattern, begins, stops in ((0, none, middle), (1, middle, end)):
         for c in loads(pattern):
             c.wait()
         if pattern == 0:
@@ -138,19 +138,19 @@
                 c.start()
         for row in range(2):
             own_blocks(pattern, row)
-
-        for width in (UNROLL, 2, 1):
-
-            def several(j, carry, pattern=pattern, begin=begin, width=width):
-                got = [fetch(pattern, begin + j * width + u) for u in range(width)]
-                scores = [score(pattern, g[0], g[1]) for g in got]
-                for g, s in zip(got, scores):
-                    absorb(pattern, s, *g)
-                return carry
-
-            turns = (stop - begin) // width
-            lax.fori_loop(0, turns, several, 0)
-            begin = begin + turns * width
+        for fetch, begin, stop in zip((fetch_pair, fetch_single), begins, stops):
+            for width in (UNROLL, 2, 1):
+
+                def several(j, carry, pattern=pattern, fetch=fetch, begin=begin, width=width):
+                    got = [fetch(pattern, begin + j * width + u) for u in range(width)]
+                    scores = [score(pattern, *g) for g in got]
+                    for g, s in zip(got, scores):
+                        absorb(pattern, s, *g)
+                    return carry
+
+                turns = (stop - begin) // width
+                lax.fori_loop(0, turns, several, 0)
+                begin = begin + turns * width
 
     lane = lax.broadcasted_iota(jnp.int32, (BLOCK_TOKENS, BLOCK_TOKENS), 1)
 
@@ -162,7 +162,7 @@
             o_ref[item, :, part] = acc_ref[item, part].astype(jnp.bfloat16)
             tops = jnp.where(lane == g, m_ref[item, part], tops)
             sums = jnp.where(lane == g, jnp.sum(l_ref[item, part], axis=1, keepdims=True), sums)
-        stat_ref[item, 0:8] = tops.T[:8] * EXP_SCALE
+        stat_ref[item, 0:8] = tops.T[:8]
         stat_ref[item, 8:16] = sums.T[:8]
         return carry
 
@@ -184,6 +184,7 @@
         scratch_shapes=[
             pltpu.SMEM((ITEMS,), jnp.int32),
             pltpu.SMEM((ITEMS * FMAX,), jnp.int32),
+            pltpu.SMEM((ITEMS + 1,), jnp.int32),
             pltpu.VMEM(q.shape, q.dtype),
             pltpu.VMEM(kv.shape, kv.dtype),
             state, state, state,

time: 90.6 us -> 89.4 us (0.987)
  Pallas kernels: 89.6 us -> 88.2 us
    pallas_call x1, Pallas kernels: 21.6 us -> 20.1 us  [attend(): pl.pallas_call(attend_kernel, in_specs=[pl.BlockSpec(memory_space=pltpu.S...]
where the time goes in v7:
time: 89.4 us; the launch traced here: 89 us
  Pallas kernels  88.2 us (99%)
    pallas_call x1, Pallas kernels, gather_all(): pl.pallas_call(gather_kernel, in_specs=[any_spec] * 6, out_specs=[any_spe...  46.4 us
    pallas_call x1, Pallas kernels, send_back(): pl.pallas_call(return_kernel, in_specs=[any_spec] * 2, out_specs=pl.Block...  21.6 us
    pallas_call x1, Pallas kernels, attend(): pl.pallas_call(attend_kernel, in_specs=[pl.BlockSpec(memory_space=pltpu.S...  20.1 us

profile of v7, /device:TPU:65, one launch (start us, length us, event | category | flops | bytes accessed | tf_op | source)
XLA Modules:
  0.0 89.0 jit_solution(4433597776898060081)
XLA Ops:
  0.0 46.4 %shard_map.64 = (bf16[2,4,256,640]{3,2,1,0:T(8,128)(2,1)S(1)}, bf16[2,32,512,128]{3,2,1,0:T(8,128)(2,1)S(1)}, s32[2,4,8,128]{3,2,1,0:T(8,128)S(1)}) custom-call(bf16[256,1280]{1,0:T(8,128)(2,1)} %q_hbm.1, bf16[256,256]{1,0:T(8,128)(2,1)} %k_hbm.1, bf16[256,256]{1,0:T(8,128)(2,1)} %v_hbm.1, s32[2,16]{1,0:T(2,128)} %owners_hbm.1, s32[64,128]{1,0:T(8,128)} %pairs_hbm.1, ...), custom_call_target="tpu_custom_call" | custom-call | tf_op jit(solution)/shard_map/pallas_call | solution.py:621
  46.4 20.1 %shard_map.65 = (bf16[16,128,640]{2,1,0:T(8,128)(2,1)S(1)}, f32[16,16,128]{2,1,0:T(8,128)S(1)}) custom-call(s32[8192]{0:T(1024)S(1)} %bitcast.1, bf16[2,4,256,640]{3,2,1,0:T(8,128)(2,1)S(1)} %get-tuple-element.11.q_in, bf16[2,32,512,128]{3,2,1,0:T(8,128)(2,1)S(1)} %get-tuple-element.12.kv_in), custom_call_target="tpu_custom_call" | custom-call | tf_op jit(solution)/shard_map/pallas_call | solution.py:176
  66.5 21.6 %shard_map.66 = bf16[128,2560]{1,0:T(8,128)(2,1)S(1)} custom-call(bf16[16,128,640]{2,1,0:T(8,128)(2,1)S(1)} %get-tuple-element.13.o_in, f32[16,16,128]{2,1,0:T(8,128)S(1)} %get-tuple-element.14.stat_in), custom_call_target="tpu_custom_call" | custom-call | tf_op jit(solution)/shard_map/pallas_call | solution.py:352
  88.2 0.8 copy.8
